TPU v7x, 512 devices: a whole 4x4x16 slice. The times are simulated.
512 devices in a mesh: grp: 16 (over y, x), shard: 32 (over z, core).
Axes of the slice: x: 4, y: 4, z: 16, core: 2. Of those that a mesh axis runs over, the one named last changes fastest.
Arguments:
- layer_input: bfloat16 [512, 128, 4096], P(('grp', 'shard')), may hold values from -6 to 6
- w_query: bfloat16 [4096, 64], replicated, may hold values from -0.01171875 to 0.01171875
- w_key: bfloat16 [4096, 64], replicated, may hold values from -0.09375 to 0.09375
- w_value: bfloat16 [4096, 64], replicated, may hold values from -0.09375 to 0.09375
- rel_bias: float32 [32], replicated, may hold values from -4 to 250
- context_grad: bfloat16 [512, 128, 64], P(('grp', 'shard')), may hold values from -1.5 to 1.5
- sign_bits: int32 [64, 3, 256], replicated, may hold values from 0 to 65535
- dither: int32 [512, 4096], P(('grp', 'shard')), may hold values from 0 to 65535
Outputs:
- mean_grad: float32 [64, 3, 4096], P('shard')
Inputs may be any that keep to these rules, and one draw needn't show every extreme that they name: `sign_bits`: each word holds 16 sign bits; bit k of word w is the sign bit of entry 16 w + k of the block.
All inputs are finite; a program needn't handle non-finite values. Where the computation divides by a largest or mean magnitude, that divisor is 1e-20 or more.
Results may differ from a plain program's by a relative error of at most 0.033.
The roundings to bfloat16 on the way count: a program that leaves them out, or rounds other values in their place, can miss the bound.
Values sent between devices are 32-bit elements; how exact they have to be, the bound alone decides.
No kernel may reach another device: no remote copies, remote signals or barrier semaphores. Data moves between devices by JAX's collectives and lax.ppermute only.
A program may use at most 64 MiB of HBM per device.

v0:
```python
import math

import jax
import jax.numpy as jnp
from jax import lax
from jax.sharding import PartitionSpec as P

LEVELS = 64


EPS = 1e-06
THRESHOLDS = (12, 16, 23, 32, 46, 64, 91)


def sylvester(side_len):
    counter = jnp.arange(side_len, dtype=jnp.int32)
    common = jnp.bitwise_and(counter[:, None], counter[None, :])
    parity = jnp.zeros((side_len, side_len), jnp.int32)
    for bit_index in range(side_len.bit_length() - 1):
        parity = parity + jnp.bitwise_and(jnp.right_shift(common, bit_index), 1)
    return (1 - 2 * (parity % 2)).astype(jnp.float32) / math.sqrt(side_len)


def decode_signs(sign_bits):
    bit_shifts = jnp.arange(16, dtype=jnp.int32)
    bit_values = jnp.bitwise_and(jnp.right_shift(sign_bits[..., None], bit_shifts), 1)
    flat_bits = bit_values.reshape(sign_bits.shape[:-1] + (sign_bits.shape[-1] * 16,))
    return 1.0 - 2.0 * flat_bits.astype(jnp.float32)


def rotate_blocks(blocks, signs, table, side_len):
    grid = (blocks * signs).reshape(blocks.shape[:-1] + (side_len, side_len))
    mixed = jnp.einsum("ab,...bc,cd->...ad", table, grid, table, precision=lax.Precision.HIGHEST)
    return mixed.reshape(blocks.shape)


def unrotate_blocks(blocks, signs, table, side_len):
    grid = blocks.reshape(blocks.shape[:-1] + (side_len, side_len))
    mixed = jnp.einsum("ab,...bc,cd->...ad", table, grid, table, precision=lax.Precision.HIGHEST)
    return mixed.reshape(blocks.shape) * signs


def bias_matrix(rel_bias, length):
    offsets = jnp.arange(-(length - 1), length, dtype=jnp.int32)
    distance = jnp.abs(offsets)
    far_bucket = jnp.full(distance.shape, 8, jnp.int32)
    for limit in THRESHOLDS:
        far_bucket = far_bucket + (distance >= limit).astype(jnp.int32)
    bucket = jnp.where(distance < 8, distance, far_bucket) + 16 * (offsets > 0).astype(jnp.int32)
    one_hot = (bucket[:, None] == jnp.arange(rel_bias.shape[0], dtype=jnp.int32)[None, :]).astype(
        jnp.float32
    )
    offset_bias = jnp.dot(one_hot, rel_bias, precision=lax.Precision.HIGHEST)
    position = jnp.arange(length, dtype=jnp.int32)
    index_table = position[None, :] - position[:, None] + (length - 1)
    return jnp.take(offset_bias, index_table)


def sync_every(grad_blocks, signs, dither_shift, table, side_len):
    rotated = rotate_blocks(grad_blocks, signs, table, side_len)
    peaks = lax.pmax(jnp.max(jnp.abs(rotated), axis=2), ("grp", "shard"))
    factor = LEVELS / (peaks + EPS)
    owned = lax.psum_scatter(
        jnp.floor(rotated * factor[..., None] + dither_shift),
        "shard",
        scatter_dimension=0,
        tiled=True,
    )
    return (owned, peaks)


def per_device(layer_input, w_query, w_key, w_value, rel_bias, context_grad, sign_bits, dither):
    inputs = layer_input[0]
    upstream = context_grad[0]
    length = inputs.shape[0]
    blocks_total = sign_bits.shape[0]
    block_len = sign_bits.shape[2] * 16
    side_len = math.isqrt(block_len)
    owned_rows = blocks_total // lax.axis_size("shard")
    count_all = float(lax.axis_size("grp") * lax.axis_size("shard"))
    table = sylvester(side_len)
    signs = decode_signs(sign_bits)
    dither_shift = (dither[0].astype(jnp.float32) + 0.5) / 65536.0
    bias_mat = bias_matrix(rel_bias, length)
    queries = jnp.dot(inputs, w_query, preferred_element_type=jnp.float32).astype(jnp.bfloat16)
    key_rows = jnp.dot(inputs, w_key, preferred_element_type=jnp.float32).astype(jnp.bfloat16)
    value_rows = jnp.dot(inputs, w_value, preferred_element_type=jnp.float32).astype(jnp.bfloat16)
    scores = jnp.dot(queries, key_rows.T, preferred_element_type=jnp.float32) + bias_mat
    top_score = jnp.max(scores, axis=1, keepdims=True)
    weights = jnp.exp(scores - top_score)
    probs = weights / jnp.sum(weights, axis=1, keepdims=True)
    probs_low = probs.astype(jnp.bfloat16)
    value_grad = jnp.dot(probs_low.T, upstream, preferred_element_type=jnp.float32).astype(
        jnp.bfloat16
    )

    def project(grad_rows):
        return jnp.dot(inputs.T, grad_rows, preferred_element_type=jnp.float32)

    prob_grad = jnp.dot(upstream, value_rows.T, preferred_element_type=jnp.float32)
    score_grad = (probs * (prob_grad - jnp.sum(probs * prob_grad, axis=1, keepdims=True))).astype(
        jnp.bfloat16
    )
    query_grad = jnp.dot(score_grad, key_rows, preferred_element_type=jnp.float32).astype(
        jnp.bfloat16
    )
    key_grad = jnp.dot(score_grad.T, queries, preferred_element_type=jnp.float32).astype(
        jnp.bfloat16
    )
    query_grad, key_grad = (query_grad, key_grad)
    grads = jnp.stack([project(query_grad), project(key_grad), project(value_grad)])
    grad_blocks = grads.reshape(3, blocks_total, block_len).transpose(1, 0, 2)
    owned_codes, all_peaks = sync_every(grad_blocks, signs, dither_shift, table, side_len)
    start_row = lax.axis_index("shard") * owned_rows
    own_peaks = lax.dynamic_slice_in_dim(all_peaks, start_row, owned_rows, 0)
    own_signs = lax.dynamic_slice_in_dim(signs, start_row, owned_rows, 0)
    step_size = ((own_peaks + EPS) / LEVELS)[..., None]
    totals = lax.psum(owned_codes, "grp")
    decoded = totals * step_size / count_all
    return unrotate_blocks(decoded, own_signs, table, side_len)


def solution(mesh):
    placed = (
        P(("grp", "shard"), None, None),
        P(),
        P(),
        P(),
        P(),
        P(("grp", "shard"), None, None),
        P(),
        P(("grp", "shard"), None),
    )
    return jax.shard_map(
        per_device, mesh=mesh, in_specs=placed, out_specs=P("shard", None, None), check_vma=False
    )
```

profile of v0, /device:TPU:32, one launch (start us, length us, event | category | flops | bytes accessed | tf_op | source)
XLA Modules:
  0.0 626.9 jit_solution(12371836274625897728)
XLA Ops:
  7.8 1.5 convolution_convert_fusion.1
  9.3 1.5 convolution_convert_fusion.2
  11.0 101.4 %gather_fusion = f32[16384]{0:T(1024)S(1)} fusion(f32[255]{0:T(256)S(1)} %bitcast.81, s32[16384]{0:T(1024)S(1)} %fusion.18), kind=kCustom, calls=%fused_computation | custom fusion | bytes 196608 | tf_op jit(solution)/shard_map/jit(_take)/gather | solution.py:56
  115.0 1.5 convolution_bitcast_fusion.1
  116.5 1.4 convolution_bitcast_fusion
  117.9 1.8 copy.33
  119.7 1.6 stack.12
  121.4 1.8 copy.34
  123.2 1.6 stack.13
  124.8 1.9 copy.35
  126.7 1.6 stack.14
  128.5 3.1 shift_right_arithmetic.86
  131.6 6.3 %copy.37 = s32[64,3,4096]{2,0,1:T(8,128)} copy(s32[64,3,4096]{0,2,1:T(8,128)} %bitcast.82) | data formatting | bytes 6291456 | tf_op jit(solution)/shard_map/shift_right_arithmetic | solution.py:26
  138.1 5.9 fusion.2
  144.0 6.1 reshape.113
  150.1 8.2 %fusion = f32[64,3,64,64]{2,3,1,0:T(8,128)S(1)} fusion(f32[64,3,64,64]{3,2,0,1:T(8,128)} %reshape.113), kind=kOutput, calls=%fused_computation.1 | convolution fusion | flops 604114944 | bytes 6291456 | tf_op jit(solution)/shard_map/ab,...bc,cd->...ad/dot_general | solution.py:33
  158.3 7.3 %abs_reduce_fusion = (f32[64,3]{1,0:T(8,128)S(1)}, f32[64,3,64,64]{3,2,1,0:T(8,128)}) fusion(f32[64,3,64,64]{2,3,1,0:T(8,128)S(1)} %fusion), kind=kOutput, calls=%fused_computation.3 | convolution fusion | flops 605687616 | bytes 6292224 | tf_op jit(solution)/shard_map/ab,...bc,cd->...ad/dot_general | solution.py:33
  165.7 7.9 %reshape.129 = f32[64,3,4096]{2,1,0:T(4,128)} reshape(f32[64,3,64,64]{3,2,1,0:T(8,128)} %get-tuple-element.12) | data formatting | bytes 6291456 | tf_op jit(solution)/shard_map/reshape | solution.py:34
  173.6 109.4 %pmax.7 = f32[64,3]{0,1:T(4,128)S(1)} all-reduce(f32[64,3]{0,1:T(4,128)S(1)} %copy.41), channel_id=1, replica_groups=mesh['grp'=16,'shard'=32] {'grp','shard'}, use_global_device_ids=true, to_apply=%region_4.5 | all-reduce | flops 192 | bytes 1536 | tf_op jit(solution)/shard_map/pmax | solution.py:61
  283.1 5.7 fusion.4
  290.7 206.8 %all-reduce.6.cloned.1.call-done = f32[64,3,4096]{2,0,1:T(8,128)} async-done(((f32[64,3,4096]{2,0,1:T(8,128)}), f32[64,3,4096]{2,0,1:T(8,128)}) %all-reduce.6.cloned.1.call-update) | async-done | bytes 3145744
  497.5 1.7 constant_dynamic-slice_fusion
  499.3 117.1 %all-reduce.4.cloned.1.call-done = f32[2,3,4096]{2,0,1:T(2,128)} async-done(((f32[2,3,4096]{2,0,1:T(2,128)}), f32[2,3,4096]{2,0,1:T(2,128)}) %all-reduce.4.cloned.1.call-update) | async-done | bytes 98320 | tf_op jit(solution)/shard_map/psum | solution.py:118
  618.4 1.7 dynamic-slice_multiply_fusion
  (42 shorter events, 7.7 us)
Async XLA Ops:
  6.5 1.2 copy-start
  6.5 4.3 copy-start.7
  6.5 491.0 %all-reduce.6.cloned.1.call-start = ((), (), s32[]{:S(2)}) async-start(), calls=%async_computation.1 | async-start | bytes 6291456
  11.0 101.8 %copy-start.3 = (bf16[4096,64]{0,1:T(8,128)(2,1)S(1)}, bf16[4096,64]{0,1:T(8,128)(2,1)}, u32[]{:S(2)}) copy-start(bf16[4096,64]{0,1:T(8,128)(2,1)} %param.11) | copy-start | bytes 1572868
  11.0 101.8 %copy-start.5 = (bf16[1,128,64]{1,2,0:T(8,128)(2,1)S(1)}, bf16[1,128,64]{1,2,0:T(8,128)(2,1)}, u32[]{:S(2)}) copy-start(bf16[1,128,64]{1,2,0:T(8,128)(2,1)} %param.13) | copy-start | bytes 49156
  124.8 3.5 copy-start.4
  131.6 6.5 %copy-start.1 = (f32[1,64,4096]{2,1,0:T(8,128)S(1)}, f32[1,64,4096]{2,1,0:T(8,128)}, u32[]{:S(2)}) copy-start(f32[1,64,4096]{2,1,0:T(8,128)} %stack.12) | copy-start | bytes 3145732
  131.6 6.5 %copy-start.2 = (f32[1,64,4096]{2,1,0:T(8,128)S(1)}, f32[1,64,4096]{2,1,0:T(8,128)}, u32[]{:S(2)}) copy-start(f32[1,64,4096]{2,1,0:T(8,128)} %stack.13) | copy-start | bytes 3145732
  165.7 117.4 %copy-start.6 = (s32[1,4096]{1,0:T(1,128)S(1)}, s32[1,4096]{1,0:T(1,128)}, u32[]{:S(2)}) copy-start(s32[1,4096]{1,0:T(1,128)} %param.15) | copy-start | bytes 49156
  288.8 327.6 %all-reduce.4.cloned.1.call-start = ((), (), s32[]{:S(2)}) async-start(), calls=%async_computation | async-start | bytes 196608 | tf_op jit(solution)/shard_map/psum | solution.py:118
Sparse Core Ops, SparseCore 0:
  288.9 208.5 all-reduce.5
  501.1 115.2 all-reduce.3
where the time goes:
time: 628 us; the launch traced here: 627 us
  waiting for transfers between devices  324 us (52%)
  local copies, waits for them, and re-layouts  140 us (22%)
  blocking collectives  109 us (17%)
  matrix products  24.7 us (4%)
  other arithmetic  14.5 us (2%)
  between operations  14.2 us (2%)
    unnamed x3, waiting for transfers between devices  207 us
    psum x1, waiting for transfers between devices, per_device(): totals = lax.psum(owned_codes, 'grp')  117 us
    pmax x1, blocking collectives, sync_every(): peaks = lax.pmax(jnp.max(jnp.abs(rotated), axis=2), ('grp', 'shard'))  109 us
    gather x2, local copies, waits for them, and re-layouts, bias_matrix(): return jnp.take(offset_bias, index_table)  102 us
    dot_general x2, matrix products, rotate_blocks(): jnp.einsum('ab,...bc,cd->...ad', table, grid, table, precision=lax.Precis...  15.6 us
  transfers between devices with their start and end apart: 2, of which 2 were waited for; matrix products, arithmetic and copies ran while one was open for 0% of the time, Pallas kernels for 0%

commit v1 on v0

v1 whole, which is shorter than its diff:
```python
import jax
import jax.numpy as jnp
from jax import lax
from jax.experimental import pallas as pl
from jax.experimental.pallas import tpu as pltpu
from jax.sharding import PartitionSpec as P

LEVELS = 64
EPS = 1e-06
THRESHOLDS = (12, 16, 23, 32, 46, 64, 91)
SEQ, D, HD = 128, 4096, 64
SIDE = 64
GRP, ZS = 16, 16
BATCH = 512
ROWS = 3 * ZS
F32, BF16, I32 = jnp.float32, jnp.bfloat16, jnp.int32
NT = (((1,), (1,)), ((), ()))


def iota(shape, dim):
    return lax.broadcasted_iota(I32, shape, dim)


def parity(v):
    v = v ^ (v >> 4)
    v = v ^ (v >> 2)
    v = v ^ (v >> 1)
    return v & 1


def hadamard(size, swap=0):
    row, col = iota((size, size), 0), iota((size, size), 1)
    value = (1 - 2 * parity(row & col & (SIDE - 1))).astype(F32) * 0.125
    same = (row >> 6) == ((col >> 6) ^ (swap * 2))
    return jnp.where(same, value, 0.0).astype(BF16)


def mm(a, b):
    return jnp.dot(a, b, preferred_element_type=F32)


def terms(v, count):
    out = []
    for _ in range(count):
        part = v.astype(BF16)
        out.append(part)
        v = v - part.astype(F32)
    return out


def rotate(grid, left, right, count):
    mixed = sum(mm(t, right) for t in terms(grid, count))
    return sum(mm(left, t) for t in terms(mixed, count))


def grads_kernel(x_ref, wq_ref, wk_ref, wv_ref, bias_ref, ctx_ref, bits_ref, dither_ref,
                 mine_ref, send_ref, peaks_ref, words_ref, word_scr, peak_scr, bits_scr):
    shard = lax.axis_index("shard")
    core = shard & 1
    depth = shard >> 1

    for p in range(3):
        for part in (0, 1):
            bits_scr[2 * p + part] = bits_ref[p, :, part * 128:part * 128 + 128]
    rows = []
    for half in (0, 1):
        for p in range(3):
            rows.append(jnp.concatenate(
                [bits_scr[2 * p + part, pl.ds(2 * half + b, ZS, stride=4), :]
                 for b in (0, 1) for part in (0, 1)], axis=1))
    words = jnp.concatenate(rows, axis=0)
    both = jnp.concatenate([words & 255, words >> 8], axis=0).astype(F32).astype(BF16)
    row, col = iota((512, 512), 0), iota((512, 512), 1)
    source = ((col >> 6) & 1) * 256 + (col & 63) * 4 + (col >> 7)
    select = jnp.where(row == source, 1.0, 0.0).astype(BF16)
    moved = mm(both, select)
    moved = (moved[:96] + 256.0 * moved[96:]).astype(I32)
    for half in (0, 1):
        for j in range(4):
            word_scr[:, j * 256 + half * 128:j * 256 + half * 128 + 128] = (
                moved[half * 48:half * 48 + 48, j * 128:j * 128 + 128])
    for p in range(3):
        for j in range(4):
            own = word_scr[pl.ds(p * ZS + depth, 1), j * 256:j * 256 + 256]
            words_ref[p, j:j + 1, :] = jnp.where(core == 0, own[:, :128], own[:, 128:])

    shift = (dither_ref[...].astype(F32) + 0.5) * (1.0 / 65536.0)
    shift = shift.T
    shift = jnp.concatenate([shift, shift], axis=1)
    mine_ref[ROWS] = shift
    send_ref[ROWS] = shift

    acc = jnp.zeros((SEQ, 3 * HD), F32)
    step = 512
    for k in range(0, D, step):
        w = jnp.concatenate([r[k:k + step, :] for r in (wq_ref, wk_ref, wv_ref)], axis=1)
        acc = acc + mm(x_ref[:, k:k + step], w)
    q32 = acc[:, :HD].astype(BF16).astype(F32)
    k32 = acc[:, HD:2 * HD].astype(BF16).astype(F32)
    queries, keys, values = (q32.astype(BF16), k32.astype(BF16), acc[:, 2 * HD:].astype(BF16))
    upstream = ctx_ref[...]
    offset = iota((SEQ, SEQ), 1) - iota((SEQ, SEQ), 0)
    distance = jnp.abs(offset)
    bucket = jnp.minimum(distance, 8)
    for limit in THRESHOLDS:
        bucket = bucket + (distance >= limit).astype(I32)
    bucket = bucket + jnp.where(offset > 0, 16, 0)
    bias = jnp.zeros((SEQ, SEQ), F32)
    for b in range(32):
        bias = jnp.where(bucket == b, bias_ref[b], bias)
    scores = lax.dot_general(queries, keys, NT, preferred_element_type=F32) + bias
    weights = jnp.exp(scores - jnp.max(scores, axis=1, keepdims=True))
    probs = weights / jnp.sum(weights, axis=1, keepdims=True)
    prob_grad = lax.dot_general(upstream, values, NT, preferred_element_type=F32)
    score_grad = (probs * (prob_grad - jnp.sum(probs * prob_grad, axis=1, keepdims=True))).astype(BF16)
    query_grad = lax.dot_general(k32.T.astype(BF16), score_grad, NT, preferred_element_type=F32)
    key_grad = mm(q32.T.astype(BF16), score_grad)
    value_grad = mm(upstream.astype(F32).T.astype(BF16), probs.astype(BF16))
    stacked = jnp.concatenate([query_grad, key_grad, value_grad], axis=0).astype(BF16)

    left = hadamard(192)
    right = hadamard(256, core)
    bit = iota((16, 256), 0)
    for z in range(ZS):
        grid = mm(stacked, x_ref[:, 256 * z:256 * z + 256])
        signed = []
        for p in range(3):
            for j in range(4):
                line = word_scr[p * ZS + z:p * ZS + z + 1, j * 256:j * 256 + 256]
                flip = (jnp.broadcast_to(line, (16, 256)) >> bit) & 1
                part = grid[p * 64 + j * 16:p * 64 + j * 16 + 16, :]
                signed.append(jnp.where(flip == 1, -part, part))
        turned = rotate(jnp.concatenate(signed, axis=0), left, right, 2)
        for p in range(3):
            block = turned[p * 64:p * 64 + 64, :]
            mine_ref[3 * z + p] = block[:, :128]
            send_ref[3 * z + p] = block[:, 128:]
            peak_scr[3 * z + p:3 * z + p + 1, :] = jnp.max(jnp.abs(block), axis=0, keepdims=True)
    lane, line = iota((ROWS, 128), 1), iota((ROWS, 128), 0)
    for half in (0, 1):
        peaks = peak_scr[:, half * 128:half * 128 + 128]
        low = jnp.max(jnp.where(lane < 64, peaks, 0.0), axis=1, keepdims=True)
        high = jnp.max(jnp.where(lane >= 64, peaks, 0.0), axis=1, keepdims=True)
        spread = jnp.where(lane == line, low, 0.0) + jnp.where(lane - 64 == line, high, 0.0)
        packed = jnp.max(spread, axis=0, keepdims=True)
        for z in range(ZS):
            peaks_ref[2 * z + (core ^ half)] = packed


def codes_kernel(mine_ref, other_ref, peaks_ref, out_ref):
    factor = LEVELS / (jnp.max(peaks_ref[...], axis=0) + EPS)
    lane, line = iota((ROWS, 128), 1), iota((ROWS, 128), 0)
    low = jnp.sum(jnp.where(lane == line, factor, 0.0), axis=1, keepdims=True)
    high = jnp.sum(jnp.where(lane - 64 == line, factor, 0.0), axis=1, keepdims=True)
    factor = jnp.where(lane < 64, low, high)
    for t in range(ROWS):
        f = factor[t:t + 1, :]
        codes = (jnp.floor(mine_ref[t] * f + mine_ref[ROWS])
                 + jnp.floor(other_ref[t] * f + other_ref[ROWS]))
        for q in range(GRP):
            out_ref[q, t] = codes[4 * q:4 * q + 4, :]


def decode_kernel(totals_ref, peaks_ref, words_ref, out_ref, scr):
    depth = lax.axis_index("shard") >> 1
    step = (jnp.max(peaks_ref[...], axis=0) + EPS) / LEVELS
    lane = iota((1, 128), 1)
    grids, signs = [], []
    bit = iota((16, 128), 0)
    for p in range(3):
        low = jnp.sum(jnp.where(lane == 3 * depth + p, step, 0.0), axis=1, keepdims=True)
        high = jnp.sum(jnp.where(lane - 64 == 3 * depth + p, step, 0.0), axis=1, keepdims=True)
        total = jnp.concatenate([totals_ref[q, p] for q in range(GRP)], axis=0)
        grids.append(total * jnp.where(lane < 64, low, high) / BATCH)
        for j in range(4):
            word = jnp.broadcast_to(words_ref[p, j:j + 1, :], (16, 128))
            signs.append((word >> bit) & 1)
    mixed = rotate(jnp.concatenate(grids, axis=0), hadamard(192), hadamard(128), 3)
    mixed = jnp.where(jnp.concatenate(signs, axis=0) == 1, -mixed, mixed)
    for p in range(3):
        turned = mixed[64 * p:64 * p + 64, :].T
        scr[...] = jnp.concatenate([turned, turned], axis=1)
        for b in (0, 1):
            pair = [scr[pl.ds(64 * b + odd, 32, stride=2), :][:, :SIDE] for odd in (0, 1)]
            lines = jnp.concatenate(pair, axis=1)
            for r in range(32):
                out_ref[b, p:p + 1, 128 * r:128 * r + 128] = lines[r:r + 1, :]


def vmem(count):
    return [pl.BlockSpec(memory_space=pltpu.VMEM)] * count


def shaped(*shape, dtype=F32):
    return jax.ShapeDtypeStruct(shape, dtype)


PARAMS = pltpu.CompilerParams(vmem_limit_bytes=40 * 1024 * 1024)


def per_device(layer_input, w_query, w_key, w_value, rel_bias, context_grad, sign_bits, dither):
    in_specs = vmem(8)
    in_specs[4] = pl.BlockSpec(memory_space=pltpu.SMEM)
    mine, send, peaks, words = pl.pallas_call(
        grads_kernel,
        out_shape=[shaped(ROWS + 1, SIDE, 128), shaped(ROWS + 1, SIDE, 128),
                   shaped(2 * ZS, 1, 128), shaped(3, 4, 128, dtype=I32)],
        in_specs=in_specs,
        out_specs=vmem(4),
        scratch_shapes=[pltpu.VMEM((ROWS, 1024), I32), pltpu.VMEM((ROWS, 256), F32),
                        pltpu.VMEM((6, SIDE, 128), I32)],
        compiler_params=PARAMS,
        name="grads",
    )(layer_input[0], w_query, w_key, w_value, rel_bias, context_grad[0],
      sign_bits.transpose(1, 0, 2), dither.reshape(SIDE, SIDE))
    other = lax.ppermute(send, "shard", [(i, i ^ 1) for i in range(2 * ZS)])
    peaks = jnp.max(lax.all_to_all(peaks, "shard", 0, 0), axis=0)
    peaks = lax.all_to_all(jnp.broadcast_to(peaks, (GRP, 1, 128)), "grp", 0, 0)
    codes = pl.pallas_call(
        codes_kernel,
        out_shape=shaped(GRP, ROWS, 4, 128),
        in_specs=vmem(3),
        out_specs=vmem(1)[0],
        compiler_params=PARAMS,
        name="codes",
    )(mine, other, peaks)
    part = jnp.sum(lax.all_to_all(codes, "grp", 0, 0), axis=0).reshape(ZS, 3, 4, 128)
    same_core = [list(range(c, 2 * ZS, 2)) for c in (0, 1)]
    part = jnp.sum(lax.all_to_all(part, "shard", 0, 0, axis_index_groups=same_core), axis=0)
    totals = lax.all_to_all(jnp.broadcast_to(part, (GRP, 3, 4, 128)), "grp", 0, 0)
    return pl.pallas_call(
        decode_kernel,
        out_shape=shaped(2, 3, SIDE * SIDE),
        in_specs=vmem(3),
        out_specs=vmem(1)[0],
        scratch_shapes=[pltpu.VMEM((128, 128), F32)],
        compiler_params=PARAMS,
        name="decode",
    )(totals, peaks, words)


def solution(mesh):
    batch = P(("grp", "shard"), None, None)
    placed = (batch, P(), P(), P(), P(), batch, P(), P(("grp", "shard"), None))
    return jax.shard_map(
        per_device, mesh=mesh, in_specs=placed, out_specs=P("shard", None, None), check_vma=False
    )
```

time: 628 us -> 116 us (0.18)
  waiting for transfers between devices: 324 us -> 0.01 us
  local copies, waits for them, and re-layouts: 140 us -> 9.5 us
  matrix products: 24.7 us -> 0 us
  blocking collectives: 109 us -> 92 us
  between operations: 14.2 us -> 0.11 us
  other arithmetic: 14.5 us -> 1.74 us
  Pallas kernels: 0 us -> 10.2 us
    unnamed x3 -> x0, waiting for transfers between devices: 207 us -> none
    psum x1 -> x0, waiting for transfers between devices: 117 us -> none  [per_device(): totals = lax.psum(owned_codes, 'grp')]
    pmax x1 -> x0, blocking collectives: 109 us -> none  [sync_every(): peaks = lax.pmax(jnp.max(jnp.abs(rotated), axis=2), ('grp', 'shard'))]
    gather x2 -> x0, local copies, waits for them, and re-layouts: 102 us -> none  [bias_matrix(): return jnp.take(offset_bias, index_table)]
    all_to_all x0 -> x5, blocking collectives: none -> 92 us  [the longest x1 26.5 us: per_device(): peaks = jnp.max(lax.all_to_all(peaks, 'shard', 0, 0), axis=0)]
    dot_general x12 -> x0, matrix products: 24.7 us -> none  [the longest x2 15.6 us: rotate_blocks(): jnp.einsum('ab,...bc,cd->...ad', table, grid, table, precision=lax.Precis...]
    reshape x4 -> x1, local copies, waits for them, and re-layouts: 14.3 us -> 0.07 us  [per_device(): dither.reshape(SIDE, SIDE)]
    pallas_call x0 -> x3, Pallas kernels: none -> 10.2 us  [the longest x1 8.82 us: per_device(): pl.pallas_call(grads_kernel, out_shape=[shaped(ROWS + 1, SIDE, 128), shap...]
  transfers between devices with their start and end apart: 2 -> 1, of which waited for: 2 -> 0; matrix products, arithmetic and copies ran while one was open for 0% -> 0% of each run, Pallas kernels for 0% -> 0%
where the time goes in v1:
time: 116 us; the launch traced here: 115 us
  blocking collectives  92 us (79%)
  Pallas kernels  10.2 us (9%)
  local copies, waits for them, and re-layouts  9.5 us (8%)
  starting transfers between devices  1.91 us (2%)
  other arithmetic  1.74 us (2%)
    all_to_all x1, blocking collectives, per_device(): peaks = jnp.max(lax.all_to_all(peaks, 'shard', 0, 0), axis=0)  26.5 us
    all_to_all x1, blocking collectives, per_device(): lax.all_to_all(codes, 'grp', 0, 0)  24.2 us
    all_to_all x1, blocking collectives, per_device(): lax.all_to_all(part, 'shard', 0, 0, axis_index_groups=same_core)  16.4 us
    all_to_all x1, blocking collectives, per_device(): peaks = lax.all_to_all(jnp.broadcast_to(peaks, (GRP, 1, 128)), 'grp', 0, 0)  14.4 us
    all_to_all x1, blocking collectives, per_device(): lax.all_to_all(jnp.broadcast_to(part, (GRP, 3, 4, 128)), 'grp', 0, 0)  10.5 us
    pallas_call x1, Pallas kernels, per_device(): pl.pallas_call(grads_kernel, out_shape=[shaped(ROWS + 1, SIDE, 128), shap...  8.82 us
    unnamed x17, local copies, waits for them, and re-layouts  8.68 us
  transfers between devices with their start and end apart: 1, of which 0 were waited for; matrix products, arithmetic and copies ran while one was open for 0% of the time, Pallas kernels for 0%

profile of v1, /device:TPU:32, one launch (start us, length us, event | category | flops | bytes accessed | tf_op | source)
XLA Modules:
  0.0 115.5 jit_solution(11005888579975652194)
XLA Ops:
  0.0 0.5 broadcast.5
  0.5 1.4 %reduce.4 = s32[4096]{0:T(1024)S(1)} reduce(s32[1,4096]{1,0:T(1,128)} %param.15, s32[]{:T(128)} %broadcast.5), dimensions={0}, to_apply=%param.15.reduce_sub_computation.3 | reduce | bytes 32772 | tf_op args[7]
  1.9 0.1 reshape.9.dither_ref
  2.0 0.8 copy.19
  2.8 1.5 %copy.20.wq_ref = bf16[4096,64]{1,0:T(8,128)(2,1)S(1)} copy(bf16[4096,64]{0,1:T(8,128)(2,1)} %param.9) | data formatting | bytes 1048576 | tf_op args[1]
  4.4 0.0 copy-start.4
  4.4 0.5 copy.21.wk_ref
  4.9 1.5 %copy.22.wv_ref = bf16[4096,64]{1,0:T(8,128)(2,1)S(1)} copy(bf16[4096,64]{0,1:T(8,128)(2,1)} %param.11) | data formatting | bytes 1048576 | tf_op args[3]
  6.4 0.0 copy-start.2
  6.4 1.2 %copy-done.2 = bf16[1,128,4096]{2,1,0:T(8,128)(2,1)S(1)} copy-done((bf16[1,128,4096]{2,1,0:T(8,128)(2,1)S(1)}, bf16[1,128,4096]{2,1,0:T(8,128)(2,1)}, u32[]{:S(2)}) %copy-start.2) | copy-done | bytes 1048600
  7.6 8.8 %grads.1 = (f32[49,64,128]{2,1,0:T(8,128)S(1)}, f32[49,64,128]{2,1,0:T(8,128)}, f32[32,1,128]{2,1,0:T(1,128)S(1)}, s32[3,4,128]{2,1,0:T(4,128)S(1)}) custom-call(bf16[128,4096]{1,0:T(8,128)(2,1)S(1)} %bitcast.4, bf16[4096,64]{1,0:T(8,128)(2,1)S(1)} %copy.20.wq_ref, bf16[4096,64]{1,0:T(8,128)(2,1)S(1)} %copy.21.wk_ref, bf16[4096,64]{1,0:T(8,128)(2,1)S(1)} %copy.22.wv_ref, ...), custom_call_target="tpu_custom_call" | custom-call | tf_op jit(solution)/shard_map/grads/pallas_call | solution.py:204
  16.5 1.2 %copy-done = f32[49,64,128]{2,1,0:T(8,128)} copy-done((f32[49,64,128]{2,1,0:T(8,128)}, f32[49,64,128]{2,1,0:T(8,128)S(1)}, u32[]{:S(2)}) %copy-start) | copy-done | bytes 1605656
  17.6 1.9 %collective-permute-start = (f32[49,64,128]{2,1,0:T(8,128)}, f32[49,64,128]{2,1,0:T(8,128)S(1)}, u32[]{:S(2)}, u32[]{:S(2)}) collective-permute-start(f32[49,64,128]{2,1,0:T(8,128)} %get-tuple-element.10), channel_id=1, source_target_pairs={{0,1},{1,0},{2,3},{3,2},{4,5},{5,4},{6,7},{7,6},{8,9},{9,8},{10,11... | collective-permute-start | bytes 4816904 | tf_op jit(solution)/shard_map/ppermute | solution.py:216
  19.5 26.5 %all_to_all.25 = f32[32,1,128]{2,1,0:T(1,128)S(1)} all-to-all(f32[32,1,128]{2,1,0:T(1,128)S(1)} %get-tuple-element.11), channel_id=1, replica_groups=mesh['grp'=16,'shard'=32] {'shard'}, dimensions={0} | all-to-all | bytes 32768 | tf_op jit(solution)/shard_map/all_to_all | solution.py:217
  46.0 0.1 reduce_max.9
  46.1 14.4 %all_to_all.26.peaks_ref = f32[16,1,128]{2,1,0:T(1,128)S(1)} all-to-all(f32[16,1,128]{2,1,0:T(1,128)S(1)} %broadcast_in_dim.6), channel_id=1, replica_groups=mesh['grp'=16,'shard'=32] {'grp'}, dimensions={0} | all-to-all | bytes 16384 | tf_op jit(solution)/shard_map/all_to_all | solution.py:218
  60.5 1.4 %copy-done.1 = f32[49,64,128]{2,1,0:T(8,128)S(1)} copy-done((f32[49,64,128]{2,1,0:T(8,128)S(1)}, f32[49,64,128]{2,1,0:T(8,128)}, u32[]{:S(2)}) %copy-start.1) | copy-done | bytes 1605656
  61.9 0.6 codes.1
  62.5 24.2 %all_to_all.27 = f32[16,48,4,128]{3,2,1,0:T(4,128)S(1)} all-to-all(f32[16,48,4,128]{3,2,1,0:T(4,128)S(1)} %codes.1), channel_id=1, replica_groups=mesh['grp'=16,'shard'=32] {'grp'}, dimensions={0} | all-to-all | bytes 3145728 | tf_op jit(solution)/shard_map/all_to_all | solution.py:227
  86.7 0.3 reduce_sum.18
  87.0 16.4 %all_to_all.28 = f32[16,3,4,128]{3,2,1,0:T(4,128)S(1)} all-to-all(f32[16,3,4,128]{3,2,1,0:T(4,128)S(1)} %bitcast.7), channel_id=1, replica_groups={{0,2,4,6,8,10,12,14,16,18,20,22,24,26,28,30},{1,3,5,7,9,11,13,15,17,19,..., dimensions={0} | all-to-all | bytes 196608 | tf_op jit(solution)/shard_map/all_to_all | solution.py:229
  103.5 10.5 %all_to_all.29.totals_ref = f32[16,3,4,128]{3,2,1,0:T(4,128)S(1)} all-to-all(f32[16,3,4,128]{3,2,1,0:T(4,128)S(1)} %broadcast_in_dim.7), channel_id=1, replica_groups=mesh['grp'=16,'shard'=32] {'grp'}, dimensions={0} | all-to-all | bytes 196608 | tf_op jit(solution)/shard_map/all_to_all | solution.py:230
  114.0 0.8 decode.1
  114.8 0.7 copy.24
  (11 shorter events, 0.1 us)
Async XLA Ops:
  0.0 4.4 %copy-start.5 = (bf16[4096,64]{0,1:T(8,128)(2,1)S(1)}, bf16[4096,64]{0,1:T(8,128)(2,1)}, u32[]{:S(2)}) copy-start(bf16[4096,64]{0,1:T(8,128)(2,1)} %param.10) | copy-start | bytes 1572868
  4.4 2.0 %copy-start.3 = (s32[64,3,256]{2,0,1:T(8,128)S(1)}, s32[64,3,256]{2,0,1:T(8,128)}, u32[]{:S(2)}) copy-start(s32[64,3,256]{2,0,1:T(8,128)} %param.14) | copy-start | bytes 589828
  4.4 2.0 %copy-start.4 = (f32[32]{0:T(128)S(1)}, f32[32]{0:T(128)}, u32[]{:S(2)}) copy-start(f32[32]{0:T(128)} %bias_ref.1) | copy-start | bytes 388
  6.4 1.2 %copy-start.2 = (bf16[1,128,4096]{2,1,0:T(8,128)(2,1)S(1)}, bf16[1,128,4096]{2,1,0:T(8,128)(2,1)}, u32[]{:S(2)}) copy-start(bf16[1,128,4096]{2,1,0:T(8,128)(2,1)} %param.8) | copy-start | bytes 3145732
  16.5 1.2 %copy-start = (f32[49,64,128]{2,1,0:T(8,128)}, f32[49,64,128]{2,1,0:T(8,128)S(1)}, u32[]{:S(2)}) copy-start(f32[49,64,128]{2,1,0:T(8,128)S(1)} %get-tuple-element.9.mine_ref) | copy-start | bytes 4816900
  17.6 42.9 %collective-permute-start = (f32[49,64,128]{2,1,0:T(8,128)}, f32[49,64,128]{2,1,0:T(8,128)S(1)}, u32[]{:S(2)}, u32[]{:S(2)}) collective-permute-start(f32[49,64,128]{2,1,0:T(8,128)} %get-tuple-element.10), channel_id=1, source_target_pairs={{0,1},{1,0},{2,3},{3,2},{4,5},{5,4},{6,7},{7,6},{8,9},{9,8},{10,11... | collective-permute-start | bytes 4816904 | tf_op jit(solution)/shard_map/ppermute | solution.py:216
  60.5 1.4 %copy-start.1 = (f32[49,64,128]{2,1,0:T(8,128)S(1)}, f32[49,64,128]{2,1,0:T(8,128)}, u32[]{:S(2)}) copy-start(f32[49,64,128]{2,1,0:T(8,128)} %copy-done) | copy-start | bytes 4816900

commit v2 on v1

--- a/solution.py
+++ b/solution.py
@@ -13,6 +13,7 @@
 GRP, ZS = 16, 16
 BATCH = 512
 ROWS = 3 * ZS
+X_STEP = 1024
 F32, BF16, I32 = jnp.float32, jnp.bfloat16, jnp.int32
 NT = (((1,), (1,)), ((), ()))
 
@@ -53,11 +54,32 @@
     return sum(mm(left, t) for t in terms(mixed, count))
 
 
-def grads_kernel(x_ref, wq_ref, wk_ref, wv_ref, bias_ref, ctx_ref, bits_ref, dither_ref,
-                 mine_ref, send_ref, peaks_ref, words_ref, word_scr, peak_scr, bits_scr):
+def grads_kernel(x_ref, wq_ref, wk_ref, wv_ref, bias_in, ctx_in, bits_in, dither_in,
+                 mine_out, send_out, peaks_ref, words_ref, word_scr, peak_scr, bits_scr,
+                 dither_scr, grid_scr, x_scr, w_scr, bits_ref, bias_ref, dither_ref, ctx_ref,
+                 mine_ref, send_ref, x_sem, w_sem, in_sem, out_sem):
     shard = lax.axis_index("shard")
     core = shard & 1
     depth = shard >> 1
+    w_copies = [pltpu.make_async_copy(r, w_scr.at[pl.ds(HD * n, HD)], w_sem.at[n])
+                for n, r in enumerate((wq_ref, wk_ref, wv_ref))]
+    x_copies = [pltpu.make_async_copy(x_ref.at[:, pl.ds(n * X_STEP, X_STEP)],
+                                      x_scr.at[:, pl.ds(n * X_STEP, X_STEP)], x_sem.at[n])
+                for n in range(D // X_STEP)]
+    sent = []
+
+    def ship(start, count, slot):
+        rows = pl.ds(start, count)
+        for n, (src, dst) in enumerate(((mine_ref, mine_out), (send_ref, send_out))):
+            copy = pltpu.make_async_copy(src.at[rows], dst.at[rows], out_sem.at[n, slot])
+            copy.start()
+            sent.append(copy)
+
+    small = [pltpu.make_async_copy(src, dst, in_sem.at[n]) for n, (src, dst) in enumerate(
+        ((bits_in, bits_ref), (bias_in, bias_ref), (dither_in, dither_ref), (ctx_in, ctx_ref)))]
+    for copy in small + w_copies + x_copies:
+        copy.start()
+    small[0].wait()
 
     for p in range(3):
         for part in (0, 1):
@@ -84,21 +106,31 @@
             own = word_scr[pl.ds(p * ZS + depth, 1), j * 256:j * 256 + 256]
             words_ref[p, j:j + 1, :] = jnp.where(core == 0, own[:, :128], own[:, 128:])
 
-    shift = (dither_ref[...].astype(F32) + 0.5) * (1.0 / 65536.0)
-    shift = shift.T
+    for copy in small[1:]:
+        copy.wait()
+    for r in range(32):
+        dither_scr[r:r + 1, :] = dither_ref[:, 128 * r:128 * r + 128]
+    even = dither_scr[...]
+    grid_scr[pl.ds(0, 32, stride=2), :] = even
+    grid_scr[pl.ds(1, 32, stride=2), :] = pltpu.roll(even, SIDE, 1)
+    shift = ((grid_scr[...].astype(F32) + 0.5) * (1.0 / 65536.0)).T[:SIDE, :]
     shift = jnp.concatenate([shift, shift], axis=1)
     mine_ref[ROWS] = shift
     send_ref[ROWS] = shift
-
-    acc = jnp.zeros((SEQ, 3 * HD), F32)
-    step = 512
-    for k in range(0, D, step):
-        w = jnp.concatenate([r[k:k + step, :] for r in (wq_ref, wk_ref, wv_ref)], axis=1)
-        acc = acc + mm(x_ref[:, k:k + step], w)
-    q32 = acc[:, :HD].astype(BF16).astype(F32)
-    k32 = acc[:, HD:2 * HD].astype(BF16).astype(F32)
-    queries, keys, values = (q32.astype(BF16), k32.astype(BF16), acc[:, 2 * HD:].astype(BF16))
-    upstream = ctx_ref[...]
+    ship(ROWS, 1, ZS)
+
+    acc = jnp.zeros((3 * HD, SEQ), F32)
+    for copy in w_copies:
+        copy.wait()
+    for n, copy in enumerate(x_copies):
+        copy.wait()
+        for k in range(n * X_STEP, n * X_STEP + X_STEP, 512):
+            acc = acc + lax.dot_general(w_scr[:, k:k + 512], x_scr[:, k:k + 512], NT,
+                                        preferred_element_type=F32)
+    queries_t, keys_t, values_t = (acc[HD * n:HD * n + HD, :].astype(BF16) for n in range(3))
+    queries = acc[:HD, :].T.astype(BF16)
+    upstream_t = ctx_ref[...]
+    upstream = upstream_t.astype(F32).T.astype(BF16)
     offset = iota((SEQ, SEQ), 1) - iota((SEQ, SEQ), 0)
     distance = jnp.abs(offset)
     bucket = jnp.minimum(distance, 8)
@@ -108,21 +140,21 @@
     bias = jnp.zeros((SEQ, SEQ), F32)
     for b in range(32):
         bias = jnp.where(bucket == b, bias_ref[b], bias)
-    scores = lax.dot_general(queries, keys, NT, preferred_element_type=F32) + bias
+    scores = mm(queries, keys_t) + bias
     weights = jnp.exp(scores - jnp.max(scores, axis=1, keepdims=True))
     probs = weights / jnp.sum(weights, axis=1, keepdims=True)
-    prob_grad = lax.dot_general(upstream, values, NT, preferred_element_type=F32)
+    prob_grad = mm(upstream, values_t)
     score_grad = (probs * (prob_grad - jnp.sum(probs * prob_grad, axis=1, keepdims=True))).astype(BF16)
-    query_grad = lax.dot_general(k32.T.astype(BF16), score_grad, NT, preferred_element_type=F32)
-    key_grad = mm(q32.T.astype(BF16), score_grad)
-    value_grad = mm(upstream.astype(F32).T.astype(BF16), probs.astype(BF16))
+    query_grad = lax.dot_general(keys_t, score_grad, NT, preferred_element_type=F32)
+    key_grad = mm(queries_t, score_grad)
+    value_grad = mm(upstream_t, probs.astype(BF16))
     stacked = jnp.concatenate([query_grad, key_grad, value_grad], axis=0).astype(BF16)
 
     left = hadamard(192)
     right = hadamard(256, core)
     bit = iota((16, 256), 0)
     for z in range(ZS):
-        grid = mm(stacked, x_ref[:, 256 * z:256 * z + 256])
+        grid = mm(stacked, x_scr[:, 256 * z:256 * z + 256])
         signed = []
         for p in range(3):
             for j in range(4):
@@ -136,6 +168,7 @@
             mine_ref[3 * z + p] = block[:, :128]
             send_ref[3 * z + p] = block[:, 128:]
             peak_scr[3 * z + p:3 * z + p + 1, :] = jnp.max(jnp.abs(block), axis=0, keepdims=True)
+        ship(3 * z, 3, z)
     lane, line = iota((ROWS, 128), 1), iota((ROWS, 128), 0)
     for half in (0, 1):
         peaks = peak_scr[:, half * 128:half * 128 + 128]
@@ -145,6 +178,8 @@
         packed = jnp.max(spread, axis=0, keepdims=True)
         for z in range(ZS):
             peaks_ref[2 * z + (core ^ half)] = packed
+    for copy in sent:
+        copy.wait()
 
 
 def codes_kernel(mine_ref, other_ref, peaks_ref, out_ref):
@@ -184,7 +219,7 @@
             pair = [scr[pl.ds(64 * b + odd, 32, stride=2), :][:, :SIDE] for odd in (0, 1)]
             lines = jnp.concatenate(pair, axis=1)
             for r in range(32):
-                out_ref[b, p:p + 1, 128 * r:128 * r + 128] = lines[r:r + 1, :]
+                out_ref[p, b:b + 1, 128 * r:128 * r + 128] = lines[r:r + 1, :]
 
 
 def vmem(count):
@@ -195,24 +230,30 @@
     return jax.ShapeDtypeStruct(shape, dtype)
 
 
-PARAMS = pltpu.CompilerParams(vmem_limit_bytes=40 * 1024 * 1024)
+PARAMS = pltpu.CompilerParams(vmem_limit_bytes=16 * 1024 * 1024)
 
 
 def per_device(layer_input, w_query, w_key, w_value, rel_bias, context_grad, sign_bits, dither):
-    in_specs = vmem(8)
-    in_specs[4] = pl.BlockSpec(memory_space=pltpu.SMEM)
     mine, send, peaks, words = pl.pallas_call(
         grads_kernel,
         out_shape=[shaped(ROWS + 1, SIDE, 128), shaped(ROWS + 1, SIDE, 128),
                    shaped(2 * ZS, 1, 128), shaped(3, 4, 128, dtype=I32)],
-        in_specs=in_specs,
-        out_specs=vmem(4),
+        in_specs=[pl.BlockSpec(memory_space=pltpu.HBM)] * 8,
+        out_specs=[pl.BlockSpec(memory_space=pltpu.HBM)] * 2 + vmem(2),
         scratch_shapes=[pltpu.VMEM((ROWS, 1024), I32), pltpu.VMEM((ROWS, 256), F32),
-                        pltpu.VMEM((6, SIDE, 128), I32)],
-        compiler_params=PARAMS,
+                        pltpu.VMEM((6, SIDE, 128), I32),
+                        pltpu.VMEM((32, 128), I32), pltpu.VMEM((SIDE, 128), I32),
+                        pltpu.VMEM((SEQ, D), BF16), pltpu.VMEM((3 * HD, D), BF16),
+                        pltpu.VMEM((3, SIDE, 256), I32), pltpu.SMEM((32,), F32),
+                        pltpu.VMEM((1, SIDE * SIDE), I32), pltpu.VMEM((HD, SEQ), BF16),
+                        pltpu.VMEM((ROWS + 1, SIDE, 128), F32), pltpu.VMEM((ROWS + 1, SIDE, 128), F32),
+                        pltpu.SemaphoreType.DMA((D // X_STEP,)), pltpu.SemaphoreType.DMA((3,)),
+                        pltpu.SemaphoreType.DMA((4,)),
+                        pltpu.SemaphoreType.DMA((2, ZS + 1))],
+        compiler_params=pltpu.CompilerParams(vmem_limit_bytes=58 * 1024 * 1024),
         name="grads",
-    )(layer_input[0], w_query, w_key, w_value, rel_bias, context_grad[0],
-      sign_bits.transpose(1, 0, 2), dither.reshape(SIDE, SIDE))
+    )(layer_input[0], w_query.T, w_key.T, w_value.T, rel_bias, context_grad[0].T,
+      sign_bits.transpose(1, 0, 2), dither)
     other = lax.ppermute(send, "shard", [(i, i ^ 1) for i in range(2 * ZS)])
     peaks = jnp.max(lax.all_to_all(peaks, "shard", 0, 0), axis=0)
     peaks = lax.all_to_all(jnp.broadcast_to(peaks, (GRP, 1, 128)), "grp", 0, 0)
@@ -228,15 +269,16 @@
     same_core = [list(range(c, 2 * ZS, 2)) for c in (0, 1)]
     part = jnp.sum(lax.all_to_all(part, "shard", 0, 0, axis_index_groups=same_core), axis=0)
     totals = lax.all_to_all(jnp.broadcast_to(part, (GRP, 3, 4, 128)), "grp", 0, 0)
-    return pl.pallas_call(
+    out = pl.pallas_call(
         decode_kernel,
-        out_shape=shaped(2, 3, SIDE * SIDE),
+        out_shape=shaped(3, 2, SIDE * SIDE),
         in_specs=vmem(3),
         out_specs=vmem(1)[0],
         scratch_shapes=[pltpu.VMEM((128, 128), F32)],
         compiler_params=PARAMS,
         name="decode",
     )(totals, peaks, words)
+    return out.transpose(1, 0, 2)
 
 
 def solution(mesh):

time: 116 us -> 109 us (0.940)
  local copies, waits for them, and re-layouts: 9.5 us -> 1.45 us
  Pallas kernels: 10.2 us -> 12.7 us
  other arithmetic: 1.74 us -> 0.35 us
    unnamed x17 -> x4, local copies, waits for them, and re-layouts: 8.68 us -> 1.42 us
    pallas_call x1, Pallas kernels: 8.82 us -> 10.7 us  [per_device(): pl.pallas_call(grads_kernel, out_shape=[shaped(ROWS + 1, SIDE, 128), shap...]
    unnamed x1 -> x0, other arithmetic: 1.4 us -> none
where the time goes in v2:
time: 109 us
  blocking collectives  92.2 us (85%)
  Pallas kernels  12.7 us (12%)
  starting transfers between devices  1.92 us (2%)
  local copies, waits for them, and re-layouts  1.45 us (1%)
    all_to_all x1, blocking collectives, per_device(): peaks = jnp.max(lax.all_to_all(peaks, 'shard', 0, 0), axis=0)  26.6 us
    all_to_all x1, blocking collectives, per_device(): lax.all_to_all(codes, 'grp', 0, 0)  24.2 us
    all_to_all x1, blocking collectives, per_device(): lax.all_to_all(part, 'shard', 0, 0, axis_index_groups=same_core)  16.4 us
    all_to_all x1, blocking collectives, per_device(): peaks = lax.all_to_all(jnp.broadcast_to(peaks, (GRP, 1, 128)), 'grp', 0, 0)  14.4 us
    pallas_call x1, Pallas kernels, per_device(): pl.pallas_call(grads_kernel, out_shape=[shaped(ROWS + 1, SIDE, 128), shap...  10.7 us
    all_to_all x1, blocking collectives, per_device(): lax.all_to_all(jnp.broadcast_to(part, (GRP, 3, 4, 128)), 'grp', 0, 0)  10.5 us
  transfers between devices with their start and end apart: 1, of which 0 were waited for; matrix products, arithmetic and copies ran while one was open for 0% of the time, Pallas kernels for 0%

profile of v2, /device:TPU:32, one launch (start us, length us, event | category | flops | bytes accessed | tf_op | source)
XLA Modules:
  0.0 108.6 jit_solution(10043097309702824997)
XLA Ops:
  0.0 10.7 %grads.1 = (f32[49,64,128]{2,1,0:T(8,128)}, f32[49,64,128]{2,1,0:T(8,128)}, f32[32,1,128]{2,1,0:T(1,128)}, s32[3,4,128]{2,1,0:T(4,128)}) custom-call(bf16[128,4096]{1,0:T(8,128)(2,1)} %bitcast.10, bf16[64,4096]{1,0:T(8,128)(2,1)} %bitcast.11, bf16[64,4096]{1,0:T(8,128)(2,1)} %bitcast.12, bf16[64,4096]{1,0:T(8,128)(2,1)} %bitcast.13, f32[32]{0:T(128)} %bias_in.1, ...), custom_call_target="tpu_custom_call" | custom-call | tf_op jit(solution)/shard_map/grads/pallas_call | solution.py:237
  10.7 1.9 %collective-permute-start = (f32[49,64,128]{2,1,0:T(8,128)}, f32[49,64,128]{2,1,0:T(8,128)S(1)}, u32[]{:S(2)}, u32[]{:S(2)}) collective-permute-start(f32[49,64,128]{2,1,0:T(8,128)} %get-tuple-element.10), channel_id=1, source_target_pairs={{0,1},{1,0},{2,3},{3,2},{4,5},{5,4},{6,7},{7,6},{8,9},{9,8},{10,11... | collective-permute-start | bytes 4816904 | tf_op jit(solution)/shard_map/ppermute | solution.py:257
  12.6 26.6 %all_to_all.25 = f32[32,1,128]{2,1,0:T(1,128)S(1)} all-to-all(f32[32,1,128]{2,1,0:T(1,128)} %get-tuple-element.11), channel_id=1, replica_groups=mesh['grp'=16,'shard'=32] {'shard'}, dimensions={0} | all-to-all | bytes 32768 | tf_op jit(solution)/shard_map/all_to_all | solution.py:258
  39.2 0.1 reduce_max.9
  39.3 14.4 %all_to_all.26.peaks_ref = f32[16,1,128]{2,1,0:T(1,128)S(1)} all-to-all(f32[16,1,128]{2,1,0:T(1,128)S(1)} %broadcast_in_dim.6), channel_id=1, replica_groups=mesh['grp'=16,'shard'=32] {'grp'}, dimensions={0} | all-to-all | bytes 16384 | tf_op jit(solution)/shard_map/all_to_all | solution.py:259
  53.7 0.0 collective-permute-done.other_ref
  53.7 0.0 copy-start
  53.7 1.4 %copy-done = f32[49,64,128]{2,1,0:T(8,128)S(1)} copy-done((f32[49,64,128]{2,1,0:T(8,128)S(1)}, f32[49,64,128]{2,1,0:T(8,128)}, u32[]{:S(2)}) %copy-start) | copy-done | bytes 1605656
  55.1 0.6 codes.1
  55.7 24.2 %all_to_all.27 = f32[16,48,4,128]{3,2,1,0:T(4,128)S(1)} all-to-all(f32[16,48,4,128]{3,2,1,0:T(4,128)S(1)} %codes.1), channel_id=1, replica_groups=mesh['grp'=16,'shard'=32] {'grp'}, dimensions={0} | all-to-all | bytes 3145728 | tf_op jit(solution)/shard_map/all_to_all | solution.py:268
  79.9 0.0 copy-start.1
  79.9 0.3 reduce_sum.18
  80.2 16.4 %all_to_all.28 = f32[16,3,4,128]{3,2,1,0:T(4,128)S(1)} all-to-all(f32[16,3,4,128]{3,2,1,0:T(4,128)S(1)} %bitcast.14), channel_id=1, replica_groups={{0,2,4,6,8,10,12,14,16,18,20,22,24,26,28,30},{1,3,5,7,9,11,13,15,17,19,..., dimensions={0} | all-to-all | bytes 196608 | tf_op jit(solution)/shard_map/all_to_all | solution.py:270
  96.7 10.5 %all_to_all.29.totals_ref = f32[16,3,4,128]{3,2,1,0:T(4,128)S(1)} all-to-all(f32[16,3,4,128]{3,2,1,0:T(4,128)S(1)} %broadcast_in_dim.7), channel_id=1, replica_groups=mesh['grp'=16,'shard'=32] {'grp'}, dimensions={0} | all-to-all | bytes 196608 | tf_op jit(solution)/shard_map/all_to_all | solution.py:271
  107.2 0.0 copy-done.1
  107.2 1.4 %decode.1 = f32[3,2,4096]{2,1,0:T(2,128)} custom-call(f32[16,3,4,128]{3,2,1,0:T(4,128)S(1)} %all_to_all.29.totals_ref, f32[16,1,128]{2,1,0:T(1,128)S(1)} %all_to_all.26.peaks_ref, s32[3,4,128]{2,1,0:T(4,128)S(1)} %copy-done.1), custom_call_target="tpu_custom_call" | custom-call | tf_op jit(solution)/shard_map/decode/pallas_call | solution.py:272
  (3 shorter events, 0.1 us)
Async XLA Ops:
  10.7 43.0 %collective-permute-start = (f32[49,64,128]{2,1,0:T(8,128)}, f32[49,64,128]{2,1,0:T(8,128)S(1)}, u32[]{:S(2)}, u32[]{:S(2)}) collective-permute-start(f32[49,64,128]{2,1,0:T(8,128)} %get-tuple-element.10), channel_id=1, source_target_pairs={{0,1},{1,0},{2,3},{3,2},{4,5},{5,4},{6,7},{7,6},{8,9},{9,8},{10,11... | collective-permute-start | bytes 4816904 | tf_op jit(solution)/shard_map/ppermute | solution.py:257
  53.7 1.4 %copy-start = (f32[49,64,128]{2,1,0:T(8,128)S(1)}, f32[49,64,128]{2,1,0:T(8,128)}, u32[]{:S(2)}) copy-start(f32[49,64,128]{2,1,0:T(8,128)} %get-tuple-element.9.mine_ref) | copy-start | bytes 4816900
  79.9 27.3 %copy-start.1 = (s32[3,4,128]{2,1,0:T(4,128)S(1)}, s32[3,4,128]{2,1,0:T(4,128)}, u32[]{:S(2)}) copy-start(s32[3,4,128]{2,1,0:T(4,128)} %get-tuple-element.12.words_ref) | copy-start | bytes 18436

commit v3 on v2

--- a/solution.py
+++ b/solution.py
@@ -54,27 +54,24 @@
     return sum(mm(left, t) for t in terms(mixed, count))
 
 
+def side(group, core):
+    return (group >> (2 * core)) & 1
+
+
 def grads_kernel(x_ref, wq_ref, wk_ref, wv_ref, bias_in, ctx_in, bits_in, dither_in,
-                 mine_out, send_out, peaks_ref, words_ref, word_scr, peak_scr, bits_scr,
+                 keep_ref, core_ref, near_ref, cross_ref, peaks_ref, words_ref, word_scr, peak_scr, bits_scr,
                  dither_scr, grid_scr, x_scr, w_scr, bits_ref, bias_ref, dither_ref, ctx_ref,
-                 mine_ref, send_ref, x_sem, w_sem, in_sem, out_sem):
+                 x_sem, w_sem, in_sem):
     shard = lax.axis_index("shard")
     core = shard & 1
     depth = shard >> 1
+    group = lax.axis_index("grp")
+    own_side, other_side = side(group, core), side(group, 1 - core)
     w_copies = [pltpu.make_async_copy(r, w_scr.at[pl.ds(HD * n, HD)], w_sem.at[n])
                 for n, r in enumerate((wq_ref, wk_ref, wv_ref))]
     x_copies = [pltpu.make_async_copy(x_ref.at[:, pl.ds(n * X_STEP, X_STEP)],
                                       x_scr.at[:, pl.ds(n * X_STEP, X_STEP)], x_sem.at[n])
                 for n in range(D // X_STEP)]
-    sent = []
-
-    def ship(start, count, slot):
-        rows = pl.ds(start, count)
-        for n, (src, dst) in enumerate(((mine_ref, mine_out), (send_ref, send_out))):
-            copy = pltpu.make_async_copy(src.at[rows], dst.at[rows], out_sem.at[n, slot])
-            copy.start()
-            sent.append(copy)
-
     small = [pltpu.make_async_copy(src, dst, in_sem.at[n]) for n, (src, dst) in enumerate(
         ((bits_in, bits_ref), (bias_in, bias_ref), (dither_in, dither_ref), (ctx_in, ctx_ref)))]
     for copy in small + w_copies + x_copies:
@@ -106,6 +103,11 @@
             own = word_scr[pl.ds(p * ZS + depth, 1), j * 256:j * 256 + 256]
             words_ref[p, j:j + 1, :] = jnp.where(core == 0, own[:, :128], own[:, 128:])
 
+    for half in (0, 1):
+        flipped = -jnp.where(core == half, own_side, other_side)
+        for j in (2, 3):
+            lanes = slice(j * 256 + half * 128, j * 256 + half * 128 + 128)
+            word_scr[:, lanes] = word_scr[:, lanes] ^ flipped
     for copy in small[1:]:
         copy.wait()
     for r in range(32):
@@ -115,9 +117,9 @@
     grid_scr[pl.ds(1, 32, stride=2), :] = pltpu.roll(even, SIDE, 1)
     shift = ((grid_scr[...].astype(F32) + 0.5) * (1.0 / 65536.0)).T[:SIDE, :]
     shift = jnp.concatenate([shift, shift], axis=1)
-    mine_ref[ROWS] = shift
-    send_ref[ROWS] = shift
-    ship(ROWS, 1, ZS)
+    for chosen, refs in ((own_side, (keep_ref, near_ref)), (other_side, (core_ref, cross_ref))):
+        refs[0][ROWS] = jnp.where(chosen == 0, shift[:32], shift[32:])
+        refs[1][ROWS] = jnp.where(chosen == 0, shift[32:], shift[:32])
 
     acc = jnp.zeros((3 * HD, SEQ), F32)
     for copy in w_copies:
@@ -152,23 +154,24 @@
 
     left = hadamard(192)
     right = hadamard(256, core)
-    bit = iota((16, 256), 0)
+    bit = 31 - iota((16, 256), 0)
     for z in range(ZS):
         grid = mm(stacked, x_scr[:, 256 * z:256 * z + 256])
         signed = []
         for p in range(3):
             for j in range(4):
                 line = word_scr[p * ZS + z:p * ZS + z + 1, j * 256:j * 256 + 256]
-                flip = (jnp.broadcast_to(line, (16, 256)) >> bit) & 1
+                flip = jnp.broadcast_to(line, (16, 256)) << bit
                 part = grid[p * 64 + j * 16:p * 64 + j * 16 + 16, :]
-                signed.append(jnp.where(flip == 1, -part, part))
+                signed.append(jnp.where(flip < 0, -part, part))
         turned = rotate(jnp.concatenate(signed, axis=0), left, right, 2)
         for p in range(3):
             block = turned[p * 64:p * 64 + 64, :]
-            mine_ref[3 * z + p] = block[:, :128]
-            send_ref[3 * z + p] = block[:, 128:]
+            keep_ref[3 * z + p] = block[:32, :128]
+            near_ref[3 * z + p] = block[32:, :128]
+            core_ref[3 * z + p] = block[:32, 128:]
+            cross_ref[3 * z + p] = block[32:, 128:]
             peak_scr[3 * z + p:3 * z + p + 1, :] = jnp.max(jnp.abs(block), axis=0, keepdims=True)
-        ship(3 * z, 3, z)
     lane, line = iota((ROWS, 128), 1), iota((ROWS, 128), 0)
     for half in (0, 1):
         peaks = peak_scr[:, half * 128:half * 128 + 128]
@@ -178,11 +181,9 @@
         packed = jnp.max(spread, axis=0, keepdims=True)
         for z in range(ZS):
             peaks_ref[2 * z + (core ^ half)] = packed
-    for copy in sent:
-        copy.wait()
-
-
-def codes_kernel(mine_ref, other_ref, peaks_ref, out_ref):
+
+
+def codes_kernel(keep_ref, core_ref, near_ref, cross_ref, peaks_ref, out_ref):
     factor = LEVELS / (jnp.max(peaks_ref[...], axis=0) + EPS)
     lane, line = iota((ROWS, 128), 1), iota((ROWS, 128), 0)
     low = jnp.sum(jnp.where(lane == line, factor, 0.0), axis=1, keepdims=True)
@@ -190,14 +191,27 @@
     factor = jnp.where(lane < 64, low, high)
     for t in range(ROWS):
         f = factor[t:t + 1, :]
-        codes = (jnp.floor(mine_ref[t] * f + mine_ref[ROWS])
-                 + jnp.floor(other_ref[t] * f + other_ref[ROWS]))
-        for q in range(GRP):
-            out_ref[q, t] = codes[4 * q:4 * q + 4, :]
+        codes = sum(jnp.floor(ref[t] * f + ref[ROWS])
+                    for ref in (keep_ref, core_ref, near_ref, cross_ref))
+        for q in range(8):
+            out_ref[q, 4 * t:4 * t + 4, :] = codes[4 * q:4 * q + 4, :]
+
+
+def sum_kernel(parts_ref, out_ref):
+    total = jnp.sum(parts_ref[...], axis=0)
+    for t in range(ROWS):
+        out_ref[t // 3, t % 3] = total[4 * t:4 * t + 4, :]
+
+
+def member(core, parity, k):
+    if core == 0:
+        return 4 * (k >> 1) + 2 * (k & 1) + parity
+    return 4 * (2 * (k >> 2) + parity) + (k & 3)
 
 
 def decode_kernel(totals_ref, peaks_ref, words_ref, out_ref, scr):
-    depth = lax.axis_index("shard") >> 1
+    shard = lax.axis_index("shard")
+    depth, core = shard >> 1, shard & 1
     step = (jnp.max(peaks_ref[...], axis=0) + EPS) / LEVELS
     lane = iota((1, 128), 1)
     grids, signs = [], []
@@ -205,7 +219,9 @@
     for p in range(3):
         low = jnp.sum(jnp.where(lane == 3 * depth + p, step, 0.0), axis=1, keepdims=True)
         high = jnp.sum(jnp.where(lane - 64 == 3 * depth + p, step, 0.0), axis=1, keepdims=True)
-        total = jnp.concatenate([totals_ref[q, p] for q in range(GRP)], axis=0)
+        total = jnp.concatenate([totals_ref[jnp.where(core == 0, member(0, k >> 3, k & 7),
+                                                      member(1, k >> 3, k & 7)), p]
+                                 for k in range(GRP)], axis=0)
         grids.append(total * jnp.where(lane < 64, low, high) / BATCH)
         for j in range(4):
             word = jnp.broadcast_to(words_ref[p, j:j + 1, :], (16, 128))
@@ -234,38 +250,57 @@
 
 
 def per_device(layer_input, w_query, w_key, w_value, rel_bias, context_grad, sign_bits, dither):
-    mine, send, peaks, words = pl.pallas_call(
+    def hbm(v):
+        return pltpu.with_memory_space_constraint(v, pltpu.HBM)
+
+    keep, to_core, to_near, to_cross, peaks, words = pl.pallas_call(
         grads_kernel,
-        out_shape=[shaped(ROWS + 1, SIDE, 128), shaped(ROWS + 1, SIDE, 128),
+        out_shape=[*[shaped(ROWS + 1, 32, 128)] * 4,
                    shaped(2 * ZS, 1, 128), shaped(3, 4, 128, dtype=I32)],
         in_specs=[pl.BlockSpec(memory_space=pltpu.HBM)] * 8,
-        out_specs=[pl.BlockSpec(memory_space=pltpu.HBM)] * 2 + vmem(2),
+        out_specs=vmem(6),
         scratch_shapes=[pltpu.VMEM((ROWS, 1024), I32), pltpu.VMEM((ROWS, 256), F32),
                         pltpu.VMEM((6, SIDE, 128), I32),
                         pltpu.VMEM((32, 128), I32), pltpu.VMEM((SIDE, 128), I32),
                         pltpu.VMEM((SEQ, D), BF16), pltpu.VMEM((3 * HD, D), BF16),
                         pltpu.VMEM((3, SIDE, 256), I32), pltpu.SMEM((32,), F32),
                         pltpu.VMEM((1, SIDE * SIDE), I32), pltpu.VMEM((HD, SEQ), BF16),
-                        pltpu.VMEM((ROWS + 1, SIDE, 128), F32), pltpu.VMEM((ROWS + 1, SIDE, 128), F32),
                         pltpu.SemaphoreType.DMA((D // X_STEP,)), pltpu.SemaphoreType.DMA((3,)),
-                        pltpu.SemaphoreType.DMA((4,)),
-                        pltpu.SemaphoreType.DMA((2, ZS + 1))],
-        compiler_params=pltpu.CompilerParams(vmem_limit_bytes=58 * 1024 * 1024),
+                        pltpu.SemaphoreType.DMA((4,))],
+        compiler_params=PARAMS,
         name="grads",
-    )(layer_input[0], w_query.T, w_key.T, w_value.T, rel_bias, context_grad[0].T,
-      sign_bits.transpose(1, 0, 2), dither)
-    other = lax.ppermute(send, "shard", [(i, i ^ 1) for i in range(2 * ZS)])
+    )(*(hbm(v) for v in (layer_input[0], w_query.T, w_key.T, w_value.T, rel_bias,
+                         context_grad[0].T, sign_bits.transpose(1, 0, 2), dither)))
+    devices = [(g, m) for g in range(GRP) for m in range(2 * ZS)]
+    everyone = ("grp", "shard")
+
+    def swap(values, target):
+        pairs = [(32 * g + m, 32 * t + u) for g, m in devices for t, u in (target(g, m),)]
+        return lax.ppermute(values, everyone, pairs)
+
+    near = swap(to_near, lambda g, m: (g ^ (1 << 2 * (m & 1)), m))
+    cross = swap(to_cross, lambda g, m: (g ^ (4 >> 2 * (m & 1)), m ^ 1))
+    sibling = swap(to_core, lambda g, m: (g, m ^ 1))
     peaks = jnp.max(lax.all_to_all(peaks, "shard", 0, 0), axis=0)
     peaks = lax.all_to_all(jnp.broadcast_to(peaks, (GRP, 1, 128)), "grp", 0, 0)
     codes = pl.pallas_call(
         codes_kernel,
-        out_shape=shaped(GRP, ROWS, 4, 128),
-        in_specs=vmem(3),
+        out_shape=shaped(8, ROWS * 4, 128),
+        in_specs=vmem(5),
         out_specs=vmem(1)[0],
         compiler_params=PARAMS,
         name="codes",
-    )(mine, other, peaks)
-    part = jnp.sum(lax.all_to_all(codes, "grp", 0, 0), axis=0).reshape(ZS, 3, 4, 128)
+    )(keep, sibling, near, cross, peaks)
+    coders = [[32 * member(m & 1, parity, k) + m for k in range(8)]
+              for parity in (0, 1) for m in range(2 * ZS)]
+    part = pl.pallas_call(
+        sum_kernel,
+        out_shape=shaped(ZS, 3, 4, 128),
+        in_specs=vmem(1),
+        out_specs=vmem(1)[0],
+        compiler_params=PARAMS,
+        name="sum",
+    )(lax.all_to_all(codes, everyone, 0, 0, axis_index_groups=coders))
     same_core = [list(range(c, 2 * ZS, 2)) for c in (0, 1)]
     part = jnp.sum(lax.all_to_all(part, "shard", 0, 0, axis_index_groups=same_core), axis=0)
     totals = lax.all_to_all(jnp.broadcast_to(part, (GRP, 3, 4, 128)), "grp", 0, 0)

time: 109 us -> 104 us (0.954)
  blocking collectives: 92.2 us -> 83.3 us
  starting transfers between devices: 1.92 us -> 7.58 us
  local copies, waits for them, and re-layouts: 1.45 us -> 0.03 us
    all_to_all x1, blocking collectives: 24.2 us -> 15.9 us  [per_device(): lax.all_to_all(codes, everyone, 0, 0, axis_index_groups=coders)]
    ppermute x1 -> x3, starting transfers between devices: 1.92 us -> 7.58 us  [swap(): return lax.ppermute(values, everyone, pairs)]
    unnamed x4 -> x0, local copies, waits for them, and re-layouts: 1.42 us -> none
    pallas_call x2 -> x3, Pallas kernels: 11.3 us -> 11 us  [the longest x1 10.5 us: per_device(): pl.pallas_call(grads_kernel, out_shape=[*[shaped(ROWS + 1, 32, 128)] * 4,...]
  transfers between devices with their start and end apart: 1 -> 3, of which waited for: 0 -> 0; matrix products, arithmetic and copies ran while one was open for 0% -> 0% of each run, Pallas kernels for 0% -> 0%
where the time goes in v3:
time: 104 us
  blocking collectives  83.3 us (80%)
  Pallas kernels  12.5 us (12%)
  starting transfers between devices  7.58 us (7%)
    all_to_all x1, blocking collectives, per_device(): peaks = jnp.max(lax.all_to_all(peaks, 'shard', 0, 0), axis=0)  26.4 us
    all_to_all x1, blocking collectives, per_device(): lax.all_to_all(part, 'shard', 0, 0, axis_index_groups=same_core)  16.3 us
    all_to_all x1, blocking collectives, per_device(): lax.all_to_all(codes, everyone, 0, 0, axis_index_groups=coders)  15.9 us
    all_to_all x1, blocking collectives, per_device(): peaks = lax.all_to_all(jnp.broadcast_to(peaks, (GRP, 1, 128)), 'grp', 0, 0)  14.4 us
    pallas_call x1, Pallas kernels, per_device(): pl.pallas_call(grads_kernel, out_shape=[*[shaped(ROWS + 1, 32, 128)] * 4,...  10.5 us
    all_to_all x1, blocking collectives, per_device(): lax.all_to_all(jnp.broadcast_to(part, (GRP, 3, 4, 128)), 'grp', 0, 0)  10.4 us
    ppermute x3, starting transfers between devices, swap(): return lax.ppermute(values, everyone, pairs)  7.58 us
  transfers between devices with their start and end apart: 3, of which 0 were waited for; matrix products, arithmetic and copies ran while one was open for 0% of the time, Pallas kernels for 0%

profile of v3, /device:TPU:32, one launch (start us, length us, event | category | flops | bytes accessed | tf_op | source)
XLA Modules:
  0.0 103.6 jit_solution(14010388956692568061)
XLA Ops:
  0.0 10.5 %grads.1 = (f32[49,32,128]{2,1,0:T(8,128)S(1)}, f32[49,32,128]{2,1,0:T(8,128)}, f32[49,32,128]{2,1,0:T(8,128)}, f32[49,32,128]{2,1,0:T(8,128)}, f32[32,1,128]{2,1,0:T(1,128)S(1)}, /*index=5*/s32[3,4,128]{2,1,0:T(4,128)S(1)}) custom-call(bf16[128,4096]{1,0:T(8,128)(2,1)} %bitcast.9, bf16[64,4096]{1,0:T(8,128)(2,1)} %bitcast.10, bf16[64,4096]{1,0:T(8,128)(2,1)} %bitcast.11, ...), custom_call_target="tpu_custom_call" | custom-call | tf_op jit(solution)/shard_map/grads/pallas_call | solution.py:256
  10.5 1.9 %collective-permute-start = (f32[49,32,128]{2,1,0:T(8,128)}, f32[49,32,128]{2,1,0:T(8,128)S(1)}, u32[]{:S(2)}, u32[]{:S(2)}) collective-permute-start(f32[49,32,128]{2,1,0:T(8,128)} %get-tuple-element.12), channel_id=1, source_target_pairs={{0,1},{1,0},{2,3},{3,2},{4,5},{5,4},{6,7},{7,6},{8,9},{9,8},{10,11... | collective-permute-start | bytes 2408456 | tf_op jit(solution)/shard_map/ppermute | solution.py:279
  12.4 3.4 %collective-permute-start.1 = (f32[49,32,128]{2,1,0:T(8,128)}, f32[49,32,128]{2,1,0:T(8,128)S(1)}, u32[]{:S(2)}, u32[]{:S(2)}) collective-permute-start(f32[49,32,128]{2,1,0:T(8,128)} %get-tuple-element.13), channel_id=1, source_target_pairs={{0,32},{1,129},{2,34},{3,131},{4,36},{5,133},{6,38},{7,135},{8,40}... | collective-permute-start | bytes 2408456 | tf_op jit(solution)/shard_map/ppermute | solution.py:279
  15.8 2.3 %collective-permute-start.2 = (f32[49,32,128]{2,1,0:T(8,128)}, f32[49,32,128]{2,1,0:T(8,128)S(1)}, u32[]{:S(2)}, u32[]{:S(2)}) collective-permute-start(f32[49,32,128]{2,1,0:T(8,128)} %get-tuple-element.14), channel_id=1, source_target_pairs={{0,129},{1,32},{2,131},{3,34},{4,133},{5,36},{6,135},{7,38},{8,137... | collective-permute-start | bytes 2408456 | tf_op jit(solution)/shard_map/ppermute | solution.py:279
  18.1 26.4 %all_to_all.25 = f32[32,1,128]{2,1,0:T(1,128)S(1)} all-to-all(f32[32,1,128]{2,1,0:T(1,128)S(1)} %get-tuple-element.15), channel_id=1, replica_groups=mesh['grp'=16,'shard'=32] {'shard'}, dimensions={0} | all-to-all | bytes 32768 | tf_op jit(solution)/shard_map/all_to_all | solution.py:284
  44.5 0.1 reduce_max.9
  44.5 14.4 %all_to_all.26.peaks_ref = f32[16,1,128]{2,1,0:T(1,128)S(1)} all-to-all(f32[16,1,128]{2,1,0:T(1,128)S(1)} %broadcast_in_dim.6), channel_id=1, replica_groups=mesh['grp'=16,'shard'=32] {'grp'}, dimensions={0} | all-to-all | bytes 16384 | tf_op jit(solution)/shard_map/all_to_all | solution.py:285
  58.9 0.0 collective-permute-done.core_ref
  58.9 0.0 collective-permute-done.1.near_ref
  58.9 0.0 collective-permute-done.2.cross_ref
  58.9 0.5 codes.1
  59.5 15.9 %all_to_all.27.parts_ref = f32[8,192,128]{2,1,0:T(8,128)S(1)} all-to-all(f32[8,192,128]{2,1,0:T(8,128)S(1)} %codes.1), channel_id=1, replica_groups={{0,64,128,192,256,320,384,448},{1,33,65,97,257,289,321,353},{2,66,130,1..., dimensions={0} | all-to-all | bytes 1572864 | tf_op jit(solution)/shard_map/all_to_all | solution.py:303
  75.4 16.3 %all_to_all.28 = f32[16,3,4,128]{3,2,1,0:T(4,128)S(1)} all-to-all(f32[16,3,4,128]{3,2,1,0:T(4,128)S(1)} %sum.1), channel_id=1, replica_groups={{0,2,4,6,8,10,12,14,16,18,20,22,24,26,28,30},{1,3,5,7,9,11,13,15,17,19,..., dimensions={0} | all-to-all | bytes 196608 | tf_op jit(solution)/shard_map/all_to_all | solution.py:305
  91.7 10.4 %all_to_all.29.totals_ref = f32[16,3,4,128]{3,2,1,0:T(4,128)S(1)} all-to-all(f32[16,3,4,128]{3,2,1,0:T(4,128)S(1)} %broadcast_in_dim.7), channel_id=1, replica_groups=mesh['grp'=16,'shard'=32] {'grp'}, dimensions={0} | all-to-all | bytes 196608 | tf_op jit(solution)/shard_map/all_to_all | solution.py:306
  102.1 1.4 %decode.1 = f32[3,2,4096]{2,1,0:T(2,128)} custom-call(f32[16,3,4,128]{3,2,1,0:T(4,128)S(1)} %all_to_all.29.totals_ref, f32[16,1,128]{2,1,0:T(1,128)S(1)} %all_to_all.26.peaks_ref, s32[3,4,128]{2,1,0:T(4,128)S(1)} %get-tuple-element.16.words_ref), custom_call_target="tpu_custom_call" | custom-call | tf_op jit(solution)/shard_map/decode/pallas_call | solution.py:307
  (4 shorter events, 0.1 us)
Async XLA Ops:
  10.5 48.5 %collective-permute-start = (f32[49,32,128]{2,1,0:T(8,128)}, f32[49,32,128]{2,1,0:T(8,128)S(1)}, u32[]{:S(2)}, u32[]{:S(2)}) collective-permute-start(f32[49,32,128]{2,1,0:T(8,128)} %get-tuple-element.12), channel_id=1, source_target_pairs={{0,1},{1,0},{2,3},{3,2},{4,5},{5,4},{6,7},{7,6},{8,9},{9,8},{10,11... | collective-permute-start | bytes 2408456 | tf_op jit(solution)/shard_map/ppermute | solution.py:279
  12.4 46.5 %collective-permute-start.1 = (f32[49,32,128]{2,1,0:T(8,128)}, f32[49,32,128]{2,1,0:T(8,128)S(1)}, u32[]{:S(2)}, u32[]{:S(2)}) collective-permute-start(f32[49,32,128]{2,1,0:T(8,128)} %get-tuple-element.13), channel_id=1, source_target_pairs={{0,32},{1,129},{2,34},{3,131},{4,36},{5,133},{6,38},{7,135},{8,40}... | collective-permute-start | bytes 2408456 | tf_op jit(solution)/shard_map/ppermute | solution.py:279
  15.8 43.1 %collective-permute-start.2 = (f32[49,32,128]{2,1,0:T(8,128)}, f32[49,32,128]{2,1,0:T(8,128)S(1)}, u32[]{:S(2)}, u32[]{:S(2)}) collective-permute-start(f32[49,32,128]{2,1,0:T(8,128)} %get-tuple-element.14), channel_id=1, source_target_pairs={{0,129},{1,32},{2,131},{3,34},{4,133},{5,36},{6,135},{7,38},{8,137... | collective-permute-start | bytes 2408456 | tf_op jit(solution)/shard_map/ppermute | solution.py:279

commit v4 on v3

--- a/solution.py
+++ b/solution.py
@@ -14,6 +14,7 @@
 BATCH = 512
 ROWS = 3 * ZS
 X_STEP = 1024
+SHIP = (5, 10, 13, 15)
 F32, BF16, I32 = jnp.float32, jnp.bfloat16, jnp.int32
 NT = (((1,), (1,)), ((), ()))
 
@@ -59,9 +60,9 @@
 
 
 def grads_kernel(x_ref, wq_ref, wk_ref, wv_ref, bias_in, ctx_in, bits_in, dither_in,
-                 keep_ref, core_ref, near_ref, cross_ref, peaks_ref, words_ref, word_scr, peak_scr, bits_scr,
+                 keep_ref, core_out, near_out, cross_out, peaks_ref, words_ref, word_scr, peak_scr, bits_scr,
                  dither_scr, grid_scr, x_scr, w_scr, bits_ref, bias_ref, dither_ref, ctx_ref,
-                 x_sem, w_sem, in_sem):
+                 core_ref, near_ref, cross_ref, x_sem, w_sem, in_sem, out_sem):
     shard = lax.axis_index("shard")
     core = shard & 1
     depth = shard >> 1
@@ -118,8 +119,8 @@
     shift = ((grid_scr[...].astype(F32) + 0.5) * (1.0 / 65536.0)).T[:SIDE, :]
     shift = jnp.concatenate([shift, shift], axis=1)
     for chosen, refs in ((own_side, (keep_ref, near_ref)), (other_side, (core_ref, cross_ref))):
-        refs[0][ROWS] = jnp.where(chosen == 0, shift[:32], shift[32:])
-        refs[1][ROWS] = jnp.where(chosen == 0, shift[32:], shift[:32])
+        refs[0][0] = jnp.where(chosen == 0, shift[:32], shift[32:])
+        refs[1][0] = jnp.where(chosen == 0, shift[32:], shift[:32])
 
     acc = jnp.zeros((3 * HD, SEQ), F32)
     for copy in w_copies:
@@ -155,6 +156,7 @@
     left = hadamard(192)
     right = hadamard(256, core)
     bit = 31 - iota((16, 256), 0)
+    sent, shipped = [], 0
     for z in range(ZS):
         grid = mm(stacked, x_scr[:, 256 * z:256 * z + 256])
         signed = []
@@ -164,14 +166,22 @@
                 flip = jnp.broadcast_to(line, (16, 256)) << bit
                 part = grid[p * 64 + j * 16:p * 64 + j * 16 + 16, :]
                 signed.append(jnp.where(flip < 0, -part, part))
-        turned = rotate(jnp.concatenate(signed, axis=0), left, right, 2)
+        turned = rotate(jnp.concatenate(signed, axis=0), left, right, 1)
         for p in range(3):
             block = turned[p * 64:p * 64 + 64, :]
-            keep_ref[3 * z + p] = block[:32, :128]
-            near_ref[3 * z + p] = block[32:, :128]
-            core_ref[3 * z + p] = block[:32, 128:]
-            cross_ref[3 * z + p] = block[32:, 128:]
+            keep_ref[3 * z + p + 1] = block[:32, :128]
+            near_ref[3 * z + p + 1] = block[32:, :128]
+            core_ref[3 * z + p + 1] = block[:32, 128:]
+            cross_ref[3 * z + p + 1] = block[32:, 128:]
             peak_scr[3 * z + p:3 * z + p + 1, :] = jnp.max(jnp.abs(block), axis=0, keepdims=True)
+        if z in SHIP:
+            rows = pl.ds(shipped, 3 * z + 4 - shipped)
+            for n, (src, dst) in enumerate(((core_ref, core_out), (near_ref, near_out),
+                                            (cross_ref, cross_out))):
+                sent.append(pltpu.make_async_copy(src.at[rows], dst.at[rows],
+                                                  out_sem.at[n, SHIP.index(z)]))
+                sent[-1].start()
+            shipped = 3 * z + 4
     lane, line = iota((ROWS, 128), 1), iota((ROWS, 128), 0)
     for half in (0, 1):
         peaks = peak_scr[:, half * 128:half * 128 + 128]
@@ -181,6 +191,8 @@
         packed = jnp.max(spread, axis=0, keepdims=True)
         for z in range(ZS):
             peaks_ref[2 * z + (core ^ half)] = packed
+    for copy in sent:
+        copy.wait()
 
 
 def codes_kernel(keep_ref, core_ref, near_ref, cross_ref, peaks_ref, out_ref):
@@ -191,7 +203,7 @@
     factor = jnp.where(lane < 64, low, high)
     for t in range(ROWS):
         f = factor[t:t + 1, :]
-        codes = sum(jnp.floor(ref[t] * f + ref[ROWS])
+        codes = sum(jnp.floor(ref[t + 1] * f + ref[0])
                     for ref in (keep_ref, core_ref, near_ref, cross_ref))
         for q in range(8):
             out_ref[q, 4 * t:4 * t + 4, :] = codes[4 * q:4 * q + 4, :]
@@ -258,15 +270,17 @@
         out_shape=[*[shaped(ROWS + 1, 32, 128)] * 4,
                    shaped(2 * ZS, 1, 128), shaped(3, 4, 128, dtype=I32)],
         in_specs=[pl.BlockSpec(memory_space=pltpu.HBM)] * 8,
-        out_specs=vmem(6),
+        out_specs=vmem(1) + [pl.BlockSpec(memory_space=pltpu.HBM)] * 3 + vmem(2),
         scratch_shapes=[pltpu.VMEM((ROWS, 1024), I32), pltpu.VMEM((ROWS, 256), F32),
                         pltpu.VMEM((6, SIDE, 128), I32),
                         pltpu.VMEM((32, 128), I32), pltpu.VMEM((SIDE, 128), I32),
                         pltpu.VMEM((SEQ, D), BF16), pltpu.VMEM((3 * HD, D), BF16),
                         pltpu.VMEM((3, SIDE, 256), I32), pltpu.SMEM((32,), F32),
                         pltpu.VMEM((1, SIDE * SIDE), I32), pltpu.VMEM((HD, SEQ), BF16),
+                        *[pltpu.VMEM((ROWS + 1, 32, 128), F32)] * 3,
                         pltpu.SemaphoreType.DMA((D // X_STEP,)), pltpu.SemaphoreType.DMA((3,)),
-                        pltpu.SemaphoreType.DMA((4,))],
+                        pltpu.SemaphoreType.DMA((4,)),
+                        pltpu.SemaphoreType.DMA((3, len(SHIP)))],
         compiler_params=PARAMS,
         name="grads",
     )(*(hbm(v) for v in (layer_input[0], w_query.T, w_key.T, w_value.T, rel_bias,

time: 104 us -> 102 us (0.981)
  Pallas kernels: 12.5 us -> 10.5 us
    pallas_call x1, Pallas kernels: 10.5 us -> 8.55 us  [per_device(): pl.pallas_call(grads_kernel, out_shape=[*[shaped(ROWS + 1, 32, 128)] * 4,...]
where the time goes in v4:
time: 102 us
  blocking collectives  83.3 us (82%)
  Pallas kernels  10.5 us (10%)
  starting transfers between devices  7.58 us (7%)
    all_to_all x1, blocking collectives, per_device(): peaks = jnp.max(lax.all_to_all(peaks, 'shard', 0, 0), axis=0)  26.4 us
    all_to_all x1, blocking collectives, per_device(): lax.all_to_all(part, 'shard', 0, 0, axis_index_groups=same_core)  16.3 us
    all_to_all x1, blocking collectives, per_device(): lax.all_to_all(codes, everyone, 0, 0, axis_index_groups=coders)  15.9 us
    all_to_all x1, blocking collectives, per_device(): peaks = lax.all_to_all(jnp.broadcast_to(peaks, (GRP, 1, 128)), 'grp', 0, 0)  14.4 us
    all_to_all x1, blocking collectives, per_device(): lax.all_to_all(jnp.broadcast_to(part, (GRP, 3, 4, 128)), 'grp', 0, 0)  10.4 us
    pallas_call x1, Pallas kernels, per_device(): pl.pallas_call(grads_kernel, out_shape=[*[shaped(ROWS + 1, 32, 128)] * 4,...  8.55 us
    ppermute x3, starting transfers between devices, swap(): return lax.ppermute(values, everyone, pairs)  7.58 us
  transfers between devices with their start and end apart: 3, of which 0 were waited for; matrix products, arithmetic and copies ran while one was open for 0% of the time, Pallas kernels for 0%

profile of v4, /device:TPU:32, one launch (start us, length us, event | category | flops | bytes accessed | tf_op | source)
XLA Modules:
  0.0 101.6 jit_solution(6803510351572154501)
XLA Ops:
  0.0 8.6 %grads.1 = (f32[49,32,128]{2,1,0:T(8,128)S(1)}, f32[49,32,128]{2,1,0:T(8,128)}, f32[49,32,128]{2,1,0:T(8,128)}, f32[49,32,128]{2,1,0:T(8,128)}, f32[32,1,128]{2,1,0:T(1,128)S(1)}, /*index=5*/s32[3,4,128]{2,1,0:T(4,128)S(1)}) custom-call(bf16[128,4096]{1,0:T(8,128)(2,1)} %bitcast.9, bf16[64,4096]{1,0:T(8,128)(2,1)} %bitcast.10, bf16[64,4096]{1,0:T(8,128)(2,1)} %bitcast.11, ...), custom_call_target="tpu_custom_call" | custom-call | tf_op jit(solution)/shard_map/grads/pallas_call | solution.py:268
  8.6 1.9 %collective-permute-start = (f32[49,32,128]{2,1,0:T(8,128)}, f32[49,32,128]{2,1,0:T(8,128)S(1)}, u32[]{:S(2)}, u32[]{:S(2)}) collective-permute-start(f32[49,32,128]{2,1,0:T(8,128)} %get-tuple-element.12), channel_id=1, source_target_pairs={{0,1},{1,0},{2,3},{3,2},{4,5},{5,4},{6,7},{7,6},{8,9},{9,8},{10,11... | collective-permute-start | bytes 2408456 | tf_op jit(solution)/shard_map/ppermute | solution.py:293
  10.5 3.4 %collective-permute-start.1 = (f32[49,32,128]{2,1,0:T(8,128)}, f32[49,32,128]{2,1,0:T(8,128)S(1)}, u32[]{:S(2)}, u32[]{:S(2)}) collective-permute-start(f32[49,32,128]{2,1,0:T(8,128)} %get-tuple-element.13), channel_id=1, source_target_pairs={{0,32},{1,129},{2,34},{3,131},{4,36},{5,133},{6,38},{7,135},{8,40}... | collective-permute-start | bytes 2408456 | tf_op jit(solution)/shard_map/ppermute | solution.py:293
  13.9 2.3 %collective-permute-start.2 = (f32[49,32,128]{2,1,0:T(8,128)}, f32[49,32,128]{2,1,0:T(8,128)S(1)}, u32[]{:S(2)}, u32[]{:S(2)}) collective-permute-start(f32[49,32,128]{2,1,0:T(8,128)} %get-tuple-element.14), channel_id=1, source_target_pairs={{0,129},{1,32},{2,131},{3,34},{4,133},{5,36},{6,135},{7,38},{8,137... | collective-permute-start | bytes 2408456 | tf_op jit(solution)/shard_map/ppermute | solution.py:293
  16.2 26.4 %all_to_all.25 = f32[32,1,128]{2,1,0:T(1,128)S(1)} all-to-all(f32[32,1,128]{2,1,0:T(1,128)S(1)} %get-tuple-element.15), channel_id=1, replica_groups=mesh['grp'=16,'shard'=32] {'shard'}, dimensions={0} | all-to-all | bytes 32768 | tf_op jit(solution)/shard_map/all_to_all | solution.py:298
  42.6 0.1 reduce_max.9
  42.6 14.4 %all_to_all.26.peaks_ref = f32[16,1,128]{2,1,0:T(1,128)S(1)} all-to-all(f32[16,1,128]{2,1,0:T(1,128)S(1)} %broadcast_in_dim.6), channel_id=1, replica_groups=mesh['grp'=16,'shard'=32] {'grp'}, dimensions={0} | all-to-all | bytes 16384 | tf_op jit(solution)/shard_map/all_to_all | solution.py:299
  57.0 0.0 collective-permute-done.core_ref
  57.0 0.0 collective-permute-done.1.near_ref
  57.0 0.0 collective-permute-done.2.cross_ref
  57.0 0.5 codes.1
  57.5 15.9 %all_to_all.27.parts_ref = f32[8,192,128]{2,1,0:T(8,128)S(1)} all-to-all(f32[8,192,128]{2,1,0:T(8,128)S(1)} %codes.1), channel_id=1, replica_groups={{0,64,128,192,256,320,384,448},{1,33,65,97,257,289,321,353},{2,66,130,1..., dimensions={0} | all-to-all | bytes 1572864 | tf_op jit(solution)/shard_map/all_to_all | solution.py:317
  73.4 16.3 %all_to_all.28 = f32[16,3,4,128]{3,2,1,0:T(4,128)S(1)} all-to-all(f32[16,3,4,128]{3,2,1,0:T(4,128)S(1)} %sum.1), channel_id=1, replica_groups={{0,2,4,6,8,10,12,14,16,18,20,22,24,26,28,30},{1,3,5,7,9,11,13,15,17,19,..., dimensions={0} | all-to-all | bytes 196608 | tf_op jit(solution)/shard_map/all_to_all | solution.py:319
  89.8 10.4 %all_to_all.29.totals_ref = f32[16,3,4,128]{3,2,1,0:T(4,128)S(1)} all-to-all(f32[16,3,4,128]{3,2,1,0:T(4,128)S(1)} %broadcast_in_dim.7), channel_id=1, replica_groups=mesh['grp'=16,'shard'=32] {'grp'}, dimensions={0} | all-to-all | bytes 196608 | tf_op jit(solution)/shard_map/all_to_all | solution.py:320
  100.2 1.4 %decode.1 = f32[3,2,4096]{2,1,0:T(2,128)} custom-call(f32[16,3,4,128]{3,2,1,0:T(4,128)S(1)} %all_to_all.29.totals_ref, f32[16,1,128]{2,1,0:T(1,128)S(1)} %all_to_all.26.peaks_ref, s32[3,4,128]{2,1,0:T(4,128)S(1)} %get-tuple-element.16.words_ref), custom_call_target="tpu_custom_call" | custom-call | tf_op jit(solution)/shard_map/decode/pallas_call | solution.py:321
  (4 shorter events, 0.1 us)
Async XLA Ops:
  8.6 48.5 %collective-permute-start = (f32[49,32,128]{2,1,0:T(8,128)}, f32[49,32,128]{2,1,0:T(8,128)S(1)}, u32[]{:S(2)}, u32[]{:S(2)}) collective-permute-start(f32[49,32,128]{2,1,0:T(8,128)} %get-tuple-element.12), channel_id=1, source_target_pairs={{0,1},{1,0},{2,3},{3,2},{4,5},{5,4},{6,7},{7,6},{8,9},{9,8},{10,11... | collective-permute-start | bytes 2408456 | tf_op jit(solution)/shard_map/ppermute | solution.py:293
  10.5 46.5 %collective-permute-start.1 = (f32[49,32,128]{2,1,0:T(8,128)}, f32[49,32,128]{2,1,0:T(8,128)S(1)}, u32[]{:S(2)}, u32[]{:S(2)}) collective-permute-start(f32[49,32,128]{2,1,0:T(8,128)} %get-tuple-element.13), channel_id=1, source_target_pairs={{0,32},{1,129},{2,34},{3,131},{4,36},{5,133},{6,38},{7,135},{8,40}... | collective-permute-start | bytes 2408456 | tf_op jit(solution)/shard_map/ppermute | solution.py:293
  13.9 43.1 %collective-permute-start.2 = (f32[49,32,128]{2,1,0:T(8,128)}, f32[49,32,128]{2,1,0:T(8,128)S(1)}, u32[]{:S(2)}, u32[]{:S(2)}) collective-permute-start(f32[49,32,128]{2,1,0:T(8,128)} %get-tuple-element.14), channel_id=1, source_target_pairs={{0,129},{1,32},{2,131},{3,34},{4,133},{5,36},{6,135},{7,38},{8,137... | collective-permute-start | bytes 2408456 | tf_op jit(solution)/shard_map/ppermute | solution.py:293

commit v5 on v4

--- a/solution.py
+++ b/solution.py
@@ -157,31 +157,36 @@
     right = hadamard(256, core)
     bit = 31 - iota((16, 256), 0)
     sent, shipped = [], 0
-    for z in range(ZS):
-        grid = mm(stacked, x_scr[:, 256 * z:256 * z + 256])
-        signed = []
-        for p in range(3):
-            for j in range(4):
-                line = word_scr[p * ZS + z:p * ZS + z + 1, j * 256:j * 256 + 256]
-                flip = jnp.broadcast_to(line, (16, 256)) << bit
-                part = grid[p * 64 + j * 16:p * 64 + j * 16 + 16, :]
-                signed.append(jnp.where(flip < 0, -part, part))
-        turned = rotate(jnp.concatenate(signed, axis=0), left, right, 1)
-        for p in range(3):
-            block = turned[p * 64:p * 64 + 64, :]
-            keep_ref[3 * z + p + 1] = block[:32, :128]
-            near_ref[3 * z + p + 1] = block[32:, :128]
-            core_ref[3 * z + p + 1] = block[:32, 128:]
-            cross_ref[3 * z + p + 1] = block[32:, 128:]
-            peak_scr[3 * z + p:3 * z + p + 1, :] = jnp.max(jnp.abs(block), axis=0, keepdims=True)
-        if z in SHIP:
-            rows = pl.ds(shipped, 3 * z + 4 - shipped)
-            for n, (src, dst) in enumerate(((core_ref, core_out), (near_ref, near_out),
-                                            (cross_ref, cross_out))):
-                sent.append(pltpu.make_async_copy(src.at[rows], dst.at[rows],
-                                                  out_sem.at[n, SHIP.index(z)]))
-                sent[-1].start()
-            shipped = 3 * z + 4
+    for first in range(0, ZS, 8):
+        group = range(first, first + 8)
+        grids = []
+        for z in group:
+            grid = mm(stacked, x_scr[:, 256 * z:256 * z + 256])
+            for p in range(3):
+                for j in range(4):
+                    line = word_scr[p * ZS + z:p * ZS + z + 1, j * 256:j * 256 + 256]
+                    flip = jnp.broadcast_to(line, (16, 256)) << bit
+                    part = grid[p * 64 + j * 16:p * 64 + j * 16 + 16, :]
+                    grids.append(jnp.where(flip < 0, -part, part))
+        mixed = sum(mm(t, right) for t in terms(jnp.concatenate(grids, axis=0), 1))
+        mixed = terms(mixed, 1)
+        for n, z in enumerate(group):
+            turned = sum(mm(left, t[192 * n:192 * n + 192]) for t in mixed)
+            for p in range(3):
+                block = turned[p * 64:p * 64 + 64, :]
+                keep_ref[3 * z + p + 1] = block[:32, :128]
+                near_ref[3 * z + p + 1] = block[32:, :128]
+                core_ref[3 * z + p + 1] = block[:32, 128:]
+                cross_ref[3 * z + p + 1] = block[32:, 128:]
+                peak_scr[3 * z + p:3 * z + p + 1, :] = jnp.max(jnp.abs(block), axis=0, keepdims=True)
+            if z in SHIP:
+                rows = pl.ds(shipped, 3 * z + 4 - shipped)
+                for n, (src, dst) in enumerate(((core_ref, core_out), (near_ref, near_out),
+                                                (cross_ref, cross_out))):
+                    sent.append(pltpu.make_async_copy(src.at[rows], dst.at[rows],
+                                                      out_sem.at[n, SHIP.index(z)]))
+                    sent[-1].start()
+                shipped = 3 * z + 4
     lane, line = iota((ROWS, 128), 1), iota((ROWS, 128), 0)
     for half in (0, 1):
         peaks = peak_scr[:, half * 128:half * 128 + 128]

time: 102 us -> 100 us (0.980)
  Pallas kernels: 10.5 us -> 8.48 us
    pallas_call x1, Pallas kernels: 8.55 us -> 6.5 us  [per_device(): pl.pallas_call(grads_kernel, out_shape=[*[shaped(ROWS + 1, 32, 128)] * 4,...]
where the time goes in v5:
time: 100 us; the launch traced here: 99.6 us
  blocking collectives  83.3 us (83%)
  Pallas kernels  8.48 us (8%)
  starting transfers between devices  7.58 us (8%)
    all_to_all x1, blocking collectives, per_device(): peaks = jnp.max(lax.all_to_all(peaks, 'shard', 0, 0), axis=0)  26.4 us
    all_to_all x1, blocking collectives, per_device(): lax.all_to_all(part, 'shard', 0, 0, axis_index_groups=same_core)  16.3 us
    all_to_all x1, blocking collectives, per_device(): lax.all_to_all(codes, everyone, 0, 0, axis_index_groups=coders)  15.9 us
    all_to_all x1, blocking collectives, per_device(): peaks = lax.all_to_all(jnp.broadcast_to(peaks, (GRP, 1, 128)), 'grp', 0, 0)  14.4 us
    all_to_all x1, blocking collectives, per_device(): lax.all_to_all(jnp.broadcast_to(part, (GRP, 3, 4, 128)), 'grp', 0, 0)  10.4 us
    ppermute x3, starting transfers between devices, swap(): return lax.ppermute(values, everyone, pairs)  7.58 us
    pallas_call x1, Pallas kernels, per_device(): pl.pallas_call(grads_kernel, out_shape=[*[shaped(ROWS + 1, 32, 128)] * 4,...  6.5 us
  transfers between devices with their start and end apart: 3, of which 0 were waited for; matrix products, arithmetic and copies ran while one was open for 0% of the time, Pallas kernels for 0%

profile of v5, /device:TPU:32, one launch (start us, length us, event | category | flops | bytes accessed | tf_op | source)
XLA Modules:
  0.0 99.6 jit_solution(6601499167742339468)
XLA Ops:
  0.0 6.5 %grads.1 = (f32[49,32,128]{2,1,0:T(8,128)S(1)}, f32[49,32,128]{2,1,0:T(8,128)}, f32[49,32,128]{2,1,0:T(8,128)}, f32[49,32,128]{2,1,0:T(8,128)}, f32[32,1,128]{2,1,0:T(1,128)S(1)}, /*index=5*/s32[3,4,128]{2,1,0:T(4,128)S(1)}) custom-call(bf16[128,4096]{1,0:T(8,128)(2,1)} %bitcast.9, bf16[64,4096]{1,0:T(8,128)(2,1)} %bitcast.10, bf16[64,4096]{1,0:T(8,128)(2,1)} %bitcast.11, ...), custom_call_target="tpu_custom_call" | custom-call | tf_op jit(solution)/shard_map/grads/pallas_call | solution.py:273
  6.5 1.9 %collective-permute-start = (f32[49,32,128]{2,1,0:T(8,128)}, f32[49,32,128]{2,1,0:T(8,128)S(1)}, u32[]{:S(2)}, u32[]{:S(2)}) collective-permute-start(f32[49,32,128]{2,1,0:T(8,128)} %get-tuple-element.12), channel_id=1, source_target_pairs={{0,1},{1,0},{2,3},{3,2},{4,5},{5,4},{6,7},{7,6},{8,9},{9,8},{10,11... | collective-permute-start | bytes 2408456 | tf_op jit(solution)/shard_map/ppermute | solution.py:298
  8.4 3.4 %collective-permute-start.1 = (f32[49,32,128]{2,1,0:T(8,128)}, f32[49,32,128]{2,1,0:T(8,128)S(1)}, u32[]{:S(2)}, u32[]{:S(2)}) collective-permute-start(f32[49,32,128]{2,1,0:T(8,128)} %get-tuple-element.13), channel_id=1, source_target_pairs={{0,32},{1,129},{2,34},{3,131},{4,36},{5,133},{6,38},{7,135},{8,40}... | collective-permute-start | bytes 2408456 | tf_op jit(solution)/shard_map/ppermute | solution.py:298
  11.8 2.3 %collective-permute-start.2 = (f32[49,32,128]{2,1,0:T(8,128)}, f32[49,32,128]{2,1,0:T(8,128)S(1)}, u32[]{:S(2)}, u32[]{:S(2)}) collective-permute-start(f32[49,32,128]{2,1,0:T(8,128)} %get-tuple-element.14), channel_id=1, source_target_pairs={{0,129},{1,32},{2,131},{3,34},{4,133},{5,36},{6,135},{7,38},{8,137... | collective-permute-start | bytes 2408456 | tf_op jit(solution)/shard_map/ppermute | solution.py:298
  14.1 26.4 %all_to_all.25 = f32[32,1,128]{2,1,0:T(1,128)S(1)} all-to-all(f32[32,1,128]{2,1,0:T(1,128)S(1)} %get-tuple-element.15), channel_id=1, replica_groups=mesh['grp'=16,'shard'=32] {'shard'}, dimensions={0} | all-to-all | bytes 32768 | tf_op jit(solution)/shard_map/all_to_all | solution.py:303
  40.5 0.1 reduce_max.9
  40.6 14.4 %all_to_all.26.peaks_ref = f32[16,1,128]{2,1,0:T(1,128)S(1)} all-to-all(f32[16,1,128]{2,1,0:T(1,128)S(1)} %broadcast_in_dim.6), channel_id=1, replica_groups=mesh['grp'=16,'shard'=32] {'grp'}, dimensions={0} | all-to-all | bytes 16384 | tf_op jit(solution)/shard_map/all_to_all | solution.py:304
  55.0 0.0 collective-permute-done.core_ref
  55.0 0.0 collective-permute-done.1.near_ref
  55.0 0.0 collective-permute-done.2.cross_ref
  55.0 0.5 codes.1
  55.5 15.9 %all_to_all.27.parts_ref = f32[8,192,128]{2,1,0:T(8,128)S(1)} all-to-all(f32[8,192,128]{2,1,0:T(8,128)S(1)} %codes.1), channel_id=1, replica_groups={{0,64,128,192,256,320,384,448},{1,33,65,97,257,289,321,353},{2,66,130,1..., dimensions={0} | all-to-all | bytes 1572864 | tf_op jit(solution)/shard_map/all_to_all | solution.py:322
  71.4 16.3 %all_to_all.28 = f32[16,3,4,128]{3,2,1,0:T(4,128)S(1)} all-to-all(f32[16,3,4,128]{3,2,1,0:T(4,128)S(1)} %sum.1), channel_id=1, replica_groups={{0,2,4,6,8,10,12,14,16,18,20,22,24,26,28,30},{1,3,5,7,9,11,13,15,17,19,..., dimensions={0} | all-to-all | bytes 196608 | tf_op jit(solution)/shard_map/all_to_all | solution.py:324
  87.7 10.4 %all_to_all.29.totals_ref = f32[16,3,4,128]{3,2,1,0:T(4,128)S(1)} all-to-all(f32[16,3,4,128]{3,2,1,0:T(4,128)S(1)} %broadcast_in_dim.7), channel_id=1, replica_groups=mesh['grp'=16,'shard'=32] {'grp'}, dimensions={0} | all-to-all | bytes 196608 | tf_op jit(solution)/shard_map/all_to_all | solution.py:325
  98.1 1.4 %decode.1 = f32[3,2,4096]{2,1,0:T(2,128)} custom-call(f32[16,3,4,128]{3,2,1,0:T(4,128)S(1)} %all_to_all.29.totals_ref, f32[16,1,128]{2,1,0:T(1,128)S(1)} %all_to_all.26.peaks_ref, s32[3,4,128]{2,1,0:T(4,128)S(1)} %get-tuple-element.16.words_ref), custom_call_target="tpu_custom_call" | custom-call | tf_op jit(solution)/shard_map/decode/pallas_call | solution.py:326
  (4 shorter events, 0.1 us)
Async XLA Ops:
  6.5 48.5 %collective-permute-start = (f32[49,32,128]{2,1,0:T(8,128)}, f32[49,32,128]{2,1,0:T(8,128)S(1)}, u32[]{:S(2)}, u32[]{:S(2)}) collective-permute-start(f32[49,32,128]{2,1,0:T(8,128)} %get-tuple-element.12), channel_id=1, source_target_pairs={{0,1},{1,0},{2,3},{3,2},{4,5},{5,4},{6,7},{7,6},{8,9},{9,8},{10,11... | collective-permute-start | bytes 2408456 | tf_op jit(solution)/shard_map/ppermute | solution.py:298
  8.4 46.5 %collective-permute-start.1 = (f32[49,32,128]{2,1,0:T(8,128)}, f32[49,32,128]{2,1,0:T(8,128)S(1)}, u32[]{:S(2)}, u32[]{:S(2)}) collective-permute-start(f32[49,32,128]{2,1,0:T(8,128)} %get-tuple-element.13), channel_id=1, source_target_pairs={{0,32},{1,129},{2,34},{3,131},{4,36},{5,133},{6,38},{7,135},{8,40}... | collective-permute-start | bytes 2408456 | tf_op jit(solution)/shard_map/ppermute | solution.py:298
  11.8 43.1 %collective-permute-start.2 = (f32[49,32,128]{2,1,0:T(8,128)}, f32[49,32,128]{2,1,0:T(8,128)S(1)}, u32[]{:S(2)}, u32[]{:S(2)}) collective-permute-start(f32[49,32,128]{2,1,0:T(8,128)} %get-tuple-element.14), channel_id=1, source_target_pairs={{0,129},{1,32},{2,131},{3,34},{4,133},{5,36},{6,135},{7,38},{8,137... | collective-permute-start | bytes 2408456 | tf_op jit(solution)/shard_map/ppermute | solution.py:298

commit v6 on v5

--- a/solution.py
+++ b/solution.py
@@ -157,8 +157,8 @@
     right = hadamard(256, core)
     bit = 31 - iota((16, 256), 0)
     sent, shipped = [], 0
-    for first in range(0, ZS, 8):
-        group = range(first, first + 8)
+    for first in range(0, ZS, 16):
+        group = range(first, first + 16)
         grids = []
         for z in group:
             grid = mm(stacked, x_scr[:, 256 * z:256 * z + 256])
@@ -243,7 +243,7 @@
         for j in range(4):
             word = jnp.broadcast_to(words_ref[p, j:j + 1, :], (16, 128))
             signs.append((word >> bit) & 1)
-    mixed = rotate(jnp.concatenate(grids, axis=0), hadamard(192), hadamard(128), 3)
+    mixed = rotate(jnp.concatenate(grids, axis=0), hadamard(192), hadamard(128), 2)
     mixed = jnp.where(jnp.concatenate(signs, axis=0) == 1, -mixed, mixed)
     for p in range(3):
         turned = mixed[64 * p:64 * p + 64, :].T

time: 100 us -> 99.8 us (level)
  no operation moved by 1% of the time
where the time goes in v6:
time: 99.8 us; the launch traced here: 99.4 us
  blocking collectives  83.3 us (83%)
  Pallas kernels  8.28 us (8%)
  starting transfers between devices  7.58 us (8%)
    all_to_all x1, blocking collectives, per_device(): peaks = jnp.max(lax.all_to_all(peaks, 'shard', 0, 0), axis=0)  26.4 us
    all_to_all x1, blocking collectives, per_device(): lax.all_to_all(part, 'shard', 0, 0, axis_index_groups=same_core)  16.3 us
    all_to_all x1, blocking collectives, per_device(): lax.all_to_all(codes, everyone, 0, 0, axis_index_groups=coders)  15.9 us
    all_to_all x1, blocking collectives, per_device(): peaks = lax.all_to_all(jnp.broadcast_to(peaks, (GRP, 1, 128)), 'grp', 0, 0)  14.4 us
    all_to_all x1, blocking collectives, per_device(): lax.all_to_all(jnp.broadcast_to(part, (GRP, 3, 4, 128)), 'grp', 0, 0)  10.4 us
    ppermute x3, starting transfers between devices, swap(): return lax.ppermute(values, everyone, pairs)  7.58 us
    pallas_call x1, Pallas kernels, per_device(): pl.pallas_call(grads_kernel, out_shape=[*[shaped(ROWS + 1, 32, 128)] * 4,...  6.29 us
  transfers between devices with their start and end apart: 3, of which 0 were waited for; matrix products, arithmetic and copies ran while one was open for 0% of the time, Pallas kernels for 0%

profile of v6, /device:TPU:32, one launch (start us, length us, event | category | flops | bytes accessed | tf_op | source)
XLA Modules:
  0.0 99.4 jit_solution(10538323178799843641)
XLA Ops:
  0.0 6.3 %grads.1 = (f32[49,32,128]{2,1,0:T(8,128)S(1)}, f32[49,32,128]{2,1,0:T(8,128)}, f32[49,32,128]{2,1,0:T(8,128)}, f32[49,32,128]{2,1,0:T(8,128)}, f32[32,1,128]{2,1,0:T(1,128)S(1)}, /*index=5*/s32[3,4,128]{2,1,0:T(4,128)S(1)}) custom-call(bf16[128,4096]{1,0:T(8,128)(2,1)} %bitcast.9, bf16[64,4096]{1,0:T(8,128)(2,1)} %bitcast.10, bf16[64,4096]{1,0:T(8,128)(2,1)} %bitcast.11, ...), custom_call_target="tpu_custom_call" | custom-call | tf_op jit(solution)/shard_map/grads/pallas_call | solution.py:273
  6.3 1.9 %collective-permute-start = (f32[49,32,128]{2,1,0:T(8,128)}, f32[49,32,128]{2,1,0:T(8,128)S(1)}, u32[]{:S(2)}, u32[]{:S(2)}) collective-permute-start(f32[49,32,128]{2,1,0:T(8,128)} %get-tuple-element.12), channel_id=1, source_target_pairs={{0,1},{1,0},{2,3},{3,2},{4,5},{5,4},{6,7},{7,6},{8,9},{9,8},{10,11... | collective-permute-start | bytes 2408456 | tf_op jit(solution)/shard_map/ppermute | solution.py:298
  8.2 3.4 %collective-permute-start.1 = (f32[49,32,128]{2,1,0:T(8,128)}, f32[49,32,128]{2,1,0:T(8,128)S(1)}, u32[]{:S(2)}, u32[]{:S(2)}) collective-permute-start(f32[49,32,128]{2,1,0:T(8,128)} %get-tuple-element.13), channel_id=1, source_target_pairs={{0,32},{1,129},{2,34},{3,131},{4,36},{5,133},{6,38},{7,135},{8,40}... | collective-permute-start | bytes 2408456 | tf_op jit(solution)/shard_map/ppermute | solution.py:298
  11.6 2.3 %collective-permute-start.2 = (f32[49,32,128]{2,1,0:T(8,128)}, f32[49,32,128]{2,1,0:T(8,128)S(1)}, u32[]{:S(2)}, u32[]{:S(2)}) collective-permute-start(f32[49,32,128]{2,1,0:T(8,128)} %get-tuple-element.14), channel_id=1, source_target_pairs={{0,129},{1,32},{2,131},{3,34},{4,133},{5,36},{6,135},{7,38},{8,137... | collective-permute-start | bytes 2408456 | tf_op jit(solution)/shard_map/ppermute | solution.py:298
  13.9 26.4 %all_to_all.25 = f32[32,1,128]{2,1,0:T(1,128)S(1)} all-to-all(f32[32,1,128]{2,1,0:T(1,128)S(1)} %get-tuple-element.15), channel_id=1, replica_groups=mesh['grp'=16,'shard'=32] {'shard'}, dimensions={0} | all-to-all | bytes 32768 | tf_op jit(solution)/shard_map/all_to_all | solution.py:303
  40.3 0.1 reduce_max.9
  40.4 14.4 %all_to_all.26.peaks_ref = f32[16,1,128]{2,1,0:T(1,128)S(1)} all-to-all(f32[16,1,128]{2,1,0:T(1,128)S(1)} %broadcast_in_dim.6), channel_id=1, replica_groups=mesh['grp'=16,'shard'=32] {'grp'}, dimensions={0} | all-to-all | bytes 16384 | tf_op jit(solution)/shard_map/all_to_all | solution.py:304
  54.8 0.0 collective-permute-done.core_ref
  54.8 0.0 collective-permute-done.1.near_ref
  54.8 0.0 collective-permute-done.2.cross_ref
  54.8 0.5 codes.1
  55.3 15.9 %all_to_all.27.parts_ref = f32[8,192,128]{2,1,0:T(8,128)S(1)} all-to-all(f32[8,192,128]{2,1,0:T(8,128)S(1)} %codes.1), channel_id=1, replica_groups={{0,64,128,192,256,320,384,448},{1,33,65,97,257,289,321,353},{2,66,130,1..., dimensions={0} | all-to-all | bytes 1572864 | tf_op jit(solution)/shard_map/all_to_all | solution.py:322
  71.2 16.3 %all_to_all.28 = f32[16,3,4,128]{3,2,1,0:T(4,128)S(1)} all-to-all(f32[16,3,4,128]{3,2,1,0:T(4,128)S(1)} %sum.1), channel_id=1, replica_groups={{0,2,4,6,8,10,12,14,16,18,20,22,24,26,28,30},{1,3,5,7,9,11,13,15,17,19,..., dimensions={0} | all-to-all | bytes 196608 | tf_op jit(solution)/shard_map/all_to_all | solution.py:324
  87.5 10.4 %all_to_all.29.totals_ref = f32[16,3,4,128]{3,2,1,0:T(4,128)S(1)} all-to-all(f32[16,3,4,128]{3,2,1,0:T(4,128)S(1)} %broadcast_in_dim.7), channel_id=1, replica_groups=mesh['grp'=16,'shard'=32] {'grp'}, dimensions={0} | all-to-all | bytes 196608 | tf_op jit(solution)/shard_map/all_to_all | solution.py:325
  97.9 1.4 %decode.1 = f32[3,2,4096]{2,1,0:T(2,128)} custom-call(f32[16,3,4,128]{3,2,1,0:T(4,128)S(1)} %all_to_all.29.totals_ref, f32[16,1,128]{2,1,0:T(1,128)S(1)} %all_to_all.26.peaks_ref, s32[3,4,128]{2,1,0:T(4,128)S(1)} %get-tuple-element.16.words_ref), custom_call_target="tpu_custom_call" | custom-call | tf_op jit(solution)/shard_map/decode/pallas_call | solution.py:326
  (4 shorter events, 0.1 us)
Async XLA Ops:
  6.3 48.5 %collective-permute-start = (f32[49,32,128]{2,1,0:T(8,128)}, f32[49,32,128]{2,1,0:T(8,128)S(1)}, u32[]{:S(2)}, u32[]{:S(2)}) collective-permute-start(f32[49,32,128]{2,1,0:T(8,128)} %get-tuple-element.12), channel_id=1, source_target_pairs={{0,1},{1,0},{2,3},{3,2},{4,5},{5,4},{6,7},{7,6},{8,9},{9,8},{10,11... | collective-permute-start | bytes 2408456 | tf_op jit(solution)/shard_map/ppermute | solution.py:298
  8.2 46.5 %collective-permute-start.1 = (f32[49,32,128]{2,1,0:T(8,128)}, f32[49,32,128]{2,1,0:T(8,128)S(1)}, u32[]{:S(2)}, u32[]{:S(2)}) collective-permute-start(f32[49,32,128]{2,1,0:T(8,128)} %get-tuple-element.13), channel_id=1, source_target_pairs={{0,32},{1,129},{2,34},{3,131},{4,36},{5,133},{6,38},{7,135},{8,40}... | collective-permute-start | bytes 2408456 | tf_op jit(solution)/shard_map/ppermute | solution.py:298
  11.6 43.1 %collective-permute-start.2 = (f32[49,32,128]{2,1,0:T(8,128)}, f32[49,32,128]{2,1,0:T(8,128)S(1)}, u32[]{:S(2)}, u32[]{:S(2)}) collective-permute-start(f32[49,32,128]{2,1,0:T(8,128)} %get-tuple-element.14), channel_id=1, source_target_pairs={{0,129},{1,32},{2,131},{3,34},{4,133},{5,36},{6,135},{7,38},{8,137... | collective-permute-start | bytes 2408456 | tf_op jit(solution)/shard_map/ppermute | solution.py:298

commit v7 on v6

--- a/solution.py
+++ b/solution.py
@@ -14,7 +14,7 @@
 BATCH = 512
 ROWS = 3 * ZS
 X_STEP = 1024
-SHIP = (5, 10, 13, 15)
+SHIP = (6, 11, 14, 15)
 F32, BF16, I32 = jnp.float32, jnp.bfloat16, jnp.int32
 NT = (((1,), (1,)), ((), ()))
 

time: 99.8 us -> 99.8 us (level)
  no operation moved by 1% of the time
where the time goes in v7:
time: 99.8 us; the launch traced here: 99.4 us
  blocking collectives  83.3 us (83%)
  Pallas kernels  8.33 us (8%)
  starting transfers between devices  7.58 us (8%)
    all_to_all x1, blocking collectives, per_device(): peaks = jnp.max(lax.all_to_all(peaks, 'shard', 0, 0), axis=0)  26.4 us
    all_to_all x1, blocking collectives, per_device(): lax.all_to_all(part, 'shard', 0, 0, axis_index_groups=same_core)  16.3 us
    all_to_all x1, blocking collectives, per_device(): lax.all_to_all(codes, everyone, 0, 0, axis_index_groups=coders)  15.9 us
    all_to_all x1, blocking collectives, per_device(): peaks = lax.all_to_all(jnp.broadcast_to(peaks, (GRP, 1, 128)), 'grp', 0, 0)  14.4 us
    all_to_all x1, blocking collectives, per_device(): lax.all_to_all(jnp.broadcast_to(part, (GRP, 3, 4, 128)), 'grp', 0, 0)  10.4 us
    ppermute x3, starting transfers between devices, swap(): return lax.ppermute(values, everyone, pairs)  7.58 us
    pallas_call x1, Pallas kernels, per_device(): pl.pallas_call(grads_kernel, out_shape=[*[shaped(ROWS + 1, 32, 128)] * 4,...  6.35 us
  transfers between devices with their start and end apart: 3, of which 0 were waited for; matrix products, arithmetic and copies ran while one was open for 0% of the time, Pallas kernels for 0%

profile of v7, /device:TPU:32, one launch (start us, length us, event | category | flops | bytes accessed | tf_op | source)
XLA Modules:
  0.0 99.4 jit_solution(18170532727165629851)
XLA Ops:
  0.0 6.3 %grads.1 = (f32[49,32,128]{2,1,0:T(8,128)S(1)}, f32[49,32,128]{2,1,0:T(8,128)}, f32[49,32,128]{2,1,0:T(8,128)}, f32[49,32,128]{2,1,0:T(8,128)}, f32[32,1,128]{2,1,0:T(1,128)S(1)}, /*index=5*/s32[3,4,128]{2,1,0:T(4,128)S(1)}) custom-call(bf16[128,4096]{1,0:T(8,128)(2,1)} %bitcast.9, bf16[64,4096]{1,0:T(8,128)(2,1)} %bitcast.10, bf16[64,4096]{1,0:T(8,128)(2,1)} %bitcast.11, ...), custom_call_target="tpu_custom_call" | custom-call | tf_op jit(solution)/shard_map/grads/pallas_call | solution.py:273
  6.4 1.9 %collective-permute-start = (f32[49,32,128]{2,1,0:T(8,128)}, f32[49,32,128]{2,1,0:T(8,128)S(1)}, u32[]{:S(2)}, u32[]{:S(2)}) collective-permute-start(f32[49,32,128]{2,1,0:T(8,128)} %get-tuple-element.12), channel_id=1, source_target_pairs={{0,1},{1,0},{2,3},{3,2},{4,5},{5,4},{6,7},{7,6},{8,9},{9,8},{10,11... | collective-permute-start | bytes 2408456 | tf_op jit(solution)/shard_map/ppermute | solution.py:298
  8.3 3.4 %collective-permute-start.1 = (f32[49,32,128]{2,1,0:T(8,128)}, f32[49,32,128]{2,1,0:T(8,128)S(1)}, u32[]{:S(2)}, u32[]{:S(2)}) collective-permute-start(f32[49,32,128]{2,1,0:T(8,128)} %get-tuple-element.13), channel_id=1, source_target_pairs={{0,32},{1,129},{2,34},{3,131},{4,36},{5,133},{6,38},{7,135},{8,40}... | collective-permute-start | bytes 2408456 | tf_op jit(solution)/shard_map/ppermute | solution.py:298
  11.7 2.3 %collective-permute-start.2 = (f32[49,32,128]{2,1,0:T(8,128)}, f32[49,32,128]{2,1,0:T(8,128)S(1)}, u32[]{:S(2)}, u32[]{:S(2)}) collective-permute-start(f32[49,32,128]{2,1,0:T(8,128)} %get-tuple-element.14), channel_id=1, source_target_pairs={{0,129},{1,32},{2,131},{3,34},{4,133},{5,36},{6,135},{7,38},{8,137... | collective-permute-start | bytes 2408456 | tf_op jit(solution)/shard_map/ppermute | solution.py:298
  14.0 26.4 %all_to_all.25 = f32[32,1,128]{2,1,0:T(1,128)S(1)} all-to-all(f32[32,1,128]{2,1,0:T(1,128)S(1)} %get-tuple-element.15), channel_id=1, replica_groups=mesh['grp'=16,'shard'=32] {'shard'}, dimensions={0} | all-to-all | bytes 32768 | tf_op jit(solution)/shard_map/all_to_all | solution.py:303
  40.4 0.1 reduce_max.9
  40.4 14.4 %all_to_all.26.peaks_ref = f32[16,1,128]{2,1,0:T(1,128)S(1)} all-to-all(f32[16,1,128]{2,1,0:T(1,128)S(1)} %broadcast_in_dim.6), channel_id=1, replica_groups=mesh['grp'=16,'shard'=32] {'grp'}, dimensions={0} | all-to-all | bytes 16384 | tf_op jit(solution)/shard_map/all_to_all | solution.py:304
  54.8 0.0 collective-permute-done.core_ref
  54.8 0.0 collective-permute-done.1.near_ref
  54.8 0.0 collective-permute-done.2.cross_ref
  54.8 0.5 codes.1
  55.3 15.9 %all_to_all.27.parts_ref = f32[8,192,128]{2,1,0:T(8,128)S(1)} all-to-all(f32[8,192,128]{2,1,0:T(8,128)S(1)} %codes.1), channel_id=1, replica_groups={{0,64,128,192,256,320,384,448},{1,33,65,97,257,289,321,353},{2,66,130,1..., dimensions={0} | all-to-all | bytes 1572864 | tf_op jit(solution)/shard_map/all_to_all | solution.py:322
  71.2 16.3 %all_to_all.28 = f32[16,3,4,128]{3,2,1,0:T(4,128)S(1)} all-to-all(f32[16,3,4,128]{3,2,1,0:T(4,128)S(1)} %sum.1), channel_id=1, replica_groups={{0,2,4,6,8,10,12,14,16,18,20,22,24,26,28,30},{1,3,5,7,9,11,13,15,17,19,..., dimensions={0} | all-to-all | bytes 196608 | tf_op jit(solution)/shard_map/all_to_all | solution.py:324
  87.6 10.4 %all_to_all.29.totals_ref = f32[16,3,4,128]{3,2,1,0:T(4,128)S(1)} all-to-all(f32[16,3,4,128]{3,2,1,0:T(4,128)S(1)} %broadcast_in_dim.7), channel_id=1, replica_groups=mesh['grp'=16,'shard'=32] {'grp'}, dimensions={0} | all-to-all | bytes 196608 | tf_op jit(solution)/shard_map/all_to_all | solution.py:325
  98.0 1.4 %decode.1 = f32[3,2,4096]{2,1,0:T(2,128)} custom-call(f32[16,3,4,128]{3,2,1,0:T(4,128)S(1)} %all_to_all.29.totals_ref, f32[16,1,128]{2,1,0:T(1,128)S(1)} %all_to_all.26.peaks_ref, s32[3,4,128]{2,1,0:T(4,128)S(1)} %get-tuple-element.16.words_ref), custom_call_target="tpu_custom_call" | custom-call | tf_op jit(solution)/shard_map/decode/pallas_call | solution.py:326
  (4 shorter events, 0.1 us)
Async XLA Ops:
  6.4 48.5 %collective-permute-start = (f32[49,32,128]{2,1,0:T(8,128)}, f32[49,32,128]{2,1,0:T(8,128)S(1)}, u32[]{:S(2)}, u32[]{:S(2)}) collective-permute-start(f32[49,32,128]{2,1,0:T(8,128)} %get-tuple-element.12), channel_id=1, source_target_pairs={{0,1},{1,0},{2,3},{3,2},{4,5},{5,4},{6,7},{7,6},{8,9},{9,8},{10,11... | collective-permute-start | bytes 2408456 | tf_op jit(solution)/shard_map/ppermute | solution.py:298
  8.3 46.5 %collective-permute-start.1 = (f32[49,32,128]{2,1,0:T(8,128)}, f32[49,32,128]{2,1,0:T(8,128)S(1)}, u32[]{:S(2)}, u32[]{:S(2)}) collective-permute-start(f32[49,32,128]{2,1,0:T(8,128)} %get-tuple-element.13), channel_id=1, source_target_pairs={{0,32},{1,129},{2,34},{3,131},{4,36},{5,133},{6,38},{7,135},{8,40}... | collective-permute-start | bytes 2408456 | tf_op jit(solution)/shard_map/ppermute | solution.py:298
  11.7 43.1 %collective-permute-start.2 = (f32[49,32,128]{2,1,0:T(8,128)}, f32[49,32,128]{2,1,0:T(8,128)S(1)}, u32[]{:S(2)}, u32[]{:S(2)}) collective-permute-start(f32[49,32,128]{2,1,0:T(8,128)} %get-tuple-element.14), channel_id=1, source_target_pairs={{0,129},{1,32},{2,131},{3,34},{4,133},{5,36},{6,135},{7,38},{8,137... | collective-permute-start | bytes 2408456 | tf_op jit(solution)/shard_map/ppermute | solution.py:298
